TPU v7x, 32 devices: a whole 2x2x4 slice. The times are simulated.
32 devices in a mesh: row: 4 (over x, core), col: 8 (over z, y).
Axes of the slice: x: 2, y: 2, z: 4, core: 2. Of those that a mesh axis runs over, the one named last changes fastest.
Arguments:
- stem: bfloat16 [2, 512, 4096], P(None, None, ('row', 'col')), may hold values from -6 to 6
- left_pool: bfloat16 [4, 2, 512, 512], P('row'), may hold values from -0.1875 to 0.1875
- right_pool: bfloat16 [4, 2, 2, 512, 512], P('row'), may hold values from -0.1875 to 0.1875
- owners: int32 [3], replicated, may hold values from 0 to 3, as said below
- slices: int32 [3], replicated, may hold values from 0 to 1, as said below
- relabels: int32 [2, 512], replicated, may hold values from 0 to 511, each once within a row
Outputs:
- amplitudes: bfloat16 [2, 512, 4096], P(None, None, ('row', 'col'))
Inputs may be any that keep to these rules, and one draw needn't show every extreme that they name: `owners`: the 3 entries are distinct pool entries. `slices`: the 3 entries are not all equal.
All inputs are finite; a program needn't handle non-finite values.
Results may differ from a plain program's by a relative error of at most 0.0075.
Values may be sent and summed in bfloat16 or wider, within the bound.
A program may use at most 64 MiB of HBM per device.

v0:
```python
import jax
import jax.numpy as jnp
from jax import lax
from jax.sharding import PartitionSpec as P

CONTRACTIONS = 3


def broadcast(block, axis, owner):
    block = jnp.where(lax.axis_index(axis) == owner, block, jnp.zeros_like(block))
    return lax.psum(block, axis)


def complex_product(first, second):
    real = jnp.dot(first[0], second[0], preferred_element_type=jnp.float32) - jnp.dot(
        first[1], second[1], preferred_element_type=jnp.float32
    )
    imaginary = jnp.dot(first[0], second[1], preferred_element_type=jnp.float32) + jnp.dot(
        first[1], second[0], preferred_element_type=jnp.float32
    )
    return jnp.stack([real, imaginary]).astype(jnp.bfloat16)


def fetch_branch(left_pool, right_pool, root, chosen):
    left_local = left_pool[0]
    right_local = lax.dynamic_index_in_dim(right_pool[0], chosen, 0, keepdims=False)
    holder = lax.axis_index("row") == root
    local_branch = lax.cond(
        holder,
        lambda: complex_product(left_local, right_local),
        lambda: jnp.zeros(left_local.shape, jnp.bfloat16),
    )
    return broadcast(local_branch, "row", root)


def regroup_apply(blocks, worker):
    return worker(lax.all_to_all(blocks, "col", split_axis=1, concat_axis=1, tiled=True))


def body(stem, left_pool, right_pool, owners, slices, relabels):
    branches = []
    for section in range(CONTRACTIONS):
        branches.append(fetch_branch(left_pool, right_pool, owners[section], slices[section]))
    state = complex_product(branches[0], stem)
    groups = lax.axis_size("col")
    width = state.shape[1]
    for section in range(1, CONTRACTIONS):
        mapping = relabels[section - 1]
        blocks = state.reshape(2, groups, width // groups, state.shape[2])
        current = branches[section]

        def worker(piece, current=current, mapping=mapping):
            return complex_product(
                current, jnp.take(piece.reshape(2, width, piece.shape[3]), mapping, axis=1)
            )

        state = regroup_apply(blocks, worker)
    return state


def solution(mesh):
    in_specs = (
        P(None, None, ("row", "col")),
        P("row", None, None, None),
        P("row", None, None, None, None),
        P(),
        P(),
        P(),
    )
    out_specs = P(None, None, ("row", "col"))
    return jax.shard_map(body, mesh=mesh, in_specs=in_specs, out_specs=out_specs, check_vma=False)
```

profile of v0, /device:TPU:0, one launch (start us, length us, event | category | flops | bytes accessed | tf_op | source)
XLA Modules:
  0.0 146.9 jit_solution(10196046174034124460)
XLA Ops:
  6.5 0.0 all-reduce.3.cloned.1.call-start
  6.5 1.4 fusion.97
  9.8 0.1 conditional.3
  9.8 0.1 broadcast.11
  9.9 1.1 broadcast_select_fusion.2
  11.0 0.1 conditional.4
  11.0 0.1 broadcast.12
  11.1 0.0 copy-start.6
  11.1 0.9 copy-done.6
  12.0 0.1 conditional.5
  12.0 0.1 broadcast.13
  12.1 1.4 broadcast_select_fusion
  13.6 0.0 all-reduce.3.cloned.1.call-update
  13.6 0.7 copy-done.11
  14.3 80.7 %all-reduce.3.cloned.1.call-done = (bf16[2,512,512]{1,2,0:T(8,128)(2,1)}, bf16[2,512,512]{1,2,0:T(8,128)(2,1)}, bf16[2,512,512]{1,2,0:T(8,128)(2,1)}) async-done(((bf16[2,512,512]{1,2,0:T(8,128)(2,1)}, bf16[2,512,512]{1,2,0:T(8,128)(2,1)}, bf16[2,512,512]{1,2,0:T(8,128)(2,1)}), (bf16[2,512,512]{1,2,0:T(8,128)(2,1)}, bf16[2,512,512]{1,2,0:T(8,128)(2,1)}, ...) | async-done | bytes 3145744 | tf_op jit(solution)/shard_map/psum | solution.py:11
  95.0 0.0 copy-done.10
  95.0 1.5 fusion.67
  96.4 1.4 fusion.66
  97.8 1.4 fusion.54
  99.2 0.0 copy-done.9
  99.2 0.4 fusion.55
  99.6 0.0 copy-start.8
  99.6 0.7 pad_maximum_fusion.3
  100.3 5.5 %all-to-all-start = ((bf16[2,8,64,128]{3,2,0,1:T(8,128)(2,1)}), bf16[2,8,64,128]{3,2,0,1:T(8,128)(2,1)S(1)}, u32[]{:S(2)}, u32[]{:S(2)}) async-start(bf16[2,8,64,128]{3,2,0,1:T(8,128)(2,1)} %pad_maximum_fusion.3), calls=%async_computation | async-start | bytes 524288 | tf_op jit(solution)/shard_map/all_to_all | solution.py:37
  105.9 8.8 %all-to-all-done = bf16[2,8,64,128]{3,2,0,1:T(8,128)(2,1)S(1)} async-done(((bf16[2,8,64,128]{3,2,0,1:T(8,128)(2,1)}), bf16[2,8,64,128]{3,2,0,1:T(8,128)(2,1)S(1)}, u32[]{:S(2)}, u32[]{:S(2)}) %all-to-all-start) | async-done | bytes 262176 | tf_op jit(solution)/shard_map/all_to_all | solution.py:37
  114.6 0.3 copy.13
  114.9 2.1 %gather_fusion = bf16[512,2,128]{2,1,0:T(2,128)(2,1)S(1)} fusion(bf16[2,512,128]{2,0,1:T(2,128)(2,1)S(1)} %bitcast.167, s32[1024]{0:T(1024)S(1)} %pad_clamp_fusion.1), kind=kCustom, calls=%fused_computation.clone | custom fusion | bytes 526336 | tf_op jit(solution)/shard_map/jit(_take)/gather | solution.py:54
  117.0 1.8 %fusion.68 = bf16[2,512,128]{2,0,1:T(2,128)(2,1)S(1)} fusion(bf16[512,2,128]{2,1,0:T(2,128)(2,1)S(1)} %gather_fusion, pred[512]{0:T(512)(128)(4,1)S(1)} %compare_and_fusion.1), kind=kLoop, calls=%fused_computation.105 | loop fusion | flops 131072 | bytes 524800 | tf_op jit(solution)/shard_map/jit(_take)/select_n | solution.py:54
  118.8 0.4 fusion.95
  119.2 0.0 copy-done.8
  119.2 0.3 fusion.65
  119.5 0.3 fusion.64
  119.8 0.3 fusion.56
  120.2 0.3 fusion.57
  120.6 0.0 copy-start.7
  120.6 0.7 pad_maximum_fusion.4
  121.3 3.6 %all-to-all-start.1 = ((bf16[2,8,64,128]{3,2,0,1:T(8,128)(2,1)}), bf16[2,8,64,128]{3,2,0,1:T(8,128)(2,1)S(1)}, u32[]{:S(2)}, u32[]{:S(2)}) async-start(bf16[2,8,64,128]{3,2,0,1:T(8,128)(2,1)} %pad_maximum_fusion.4), calls=%async_computation.1 | async-start | bytes 524288 | tf_op jit(solution)/shard_map/all_to_all | solution.py:37
  124.9 8.5 %all-to-all-done.1 = bf16[2,8,64,128]{3,2,0,1:T(8,128)(2,1)S(1)} async-done(((bf16[2,8,64,128]{3,2,0,1:T(8,128)(2,1)}), bf16[2,8,64,128]{3,2,0,1:T(8,128)(2,1)S(1)}, u32[]{:S(2)}, u32[]{:S(2)}) %all-to-all-start.1) | async-done | bytes 262176 | tf_op jit(solution)/shard_map/all_to_all | solution.py:37
  133.4 0.3 copy.16
  133.7 2.1 %gather_fusion.1 = bf16[512,2,128]{2,1,0:T(2,128)(2,1)S(1)} fusion(bf16[2,512,128]{2,0,1:T(2,128)(2,1)S(1)} %bitcast.168, s32[1024]{0:T(1024)S(1)} %pad_clamp_fusion), kind=kCustom, calls=%fused_computation.1.clone | custom fusion | bytes 526336 | tf_op jit(solution)/shard_map/jit(_take)/gather | solution.py:54
  135.8 1.8 %fusion.69 = bf16[2,512,128]{2,0,1:T(2,128)(2,1)S(1)} fusion(bf16[512,2,128]{2,1,0:T(2,128)(2,1)S(1)} %gather_fusion.1, pred[512]{0:T(512)(128)(4,1)S(1)} %compare_and_fusion), kind=kLoop, calls=%fused_computation.106 | loop fusion | flops 131072 | bytes 524800 | tf_op jit(solution)/shard_map/jit(_take)/select_n | solution.py:54
  137.6 0.4 fusion.94
  138.0 0.0 copy-done.7
  138.0 0.3 fusion.63
  138.3 0.3 fusion.62
  138.7 0.3 fusion.61
  139.0 0.3 fusion.60
  139.4 0.7 pad_maximum_fusion.5
  (10 shorter events, 0.0 us)
Async XLA Ops:
  6.5 88.4 %all-reduce.3.cloned.1.call-start = ((), (), s32[]{:S(2)}) async-start(), calls=%async_computation.2 | async-start | bytes 6291456 | tf_op jit(solution)/shard_map/psum | solution.py:11
  11.1 1.0 copy-start.6
  13.6 0.7 copy-start.11
  13.6 81.4 %copy-start.10 = (bf16[2,512,128]{2,1,0:T(8,128)(2,1)S(1)}, bf16[2,512,128]{2,1,0:T(8,128)(2,1)}, u32[]{:S(2)}) copy-start(bf16[2,512,128]{2,1,0:T(8,128)(2,1)} %param.14) | copy-start | bytes 786436
  95.0 4.2 %copy-start.9 = (bf16[2,512,512]{1,2,0:T(8,128)(2,1)S(1)}, bf16[2,512,512]{1,2,0:T(8,128)(2,1)}, u32[]{:S(2)}) copy-start(bf16[2,512,512]{1,2,0:T(8,128)(2,1)} %get-tuple-element.155) | copy-start | bytes 3145732
  99.6 19.6 %copy-start.8 = (bf16[2,512,512]{1,2,0:T(8,128)(2,1)S(1)}, bf16[2,512,512]{1,2,0:T(8,128)(2,1)}, u32[]{:S(2)}) copy-start(bf16[2,512,512]{1,2,0:T(8,128)(2,1)} %get-tuple-element.154) | copy-start | bytes 3145732
  100.3 14.3 %all-to-all-start = ((bf16[2,8,64,128]{3,2,0,1:T(8,128)(2,1)}), bf16[2,8,64,128]{3,2,0,1:T(8,128)(2,1)S(1)}, u32[]{:S(2)}, u32[]{:S(2)}) async-start(bf16[2,8,64,128]{3,2,0,1:T(8,128)(2,1)} %pad_maximum_fusion.3), calls=%async_computation | async-start | bytes 524288 | tf_op jit(solution)/shard_map/all_to_all | solution.py:37
  120.6 17.4 %copy-start.7 = (bf16[2,512,512]{1,2,0:T(8,128)(2,1)S(1)}, bf16[2,512,512]{1,2,0:T(8,128)(2,1)}, u32[]{:S(2)}) copy-start(bf16[2,512,512]{1,2,0:T(8,128)(2,1)} %get-tuple-element.153) | copy-start | bytes 3145732
  121.3 12.2 %all-to-all-start.1 = ((bf16[2,8,64,128]{3,2,0,1:T(8,128)(2,1)}), bf16[2,8,64,128]{3,2,0,1:T(8,128)(2,1)S(1)}, u32[]{:S(2)}, u32[]{:S(2)}) async-start(bf16[2,8,64,128]{3,2,0,1:T(8,128)(2,1)} %pad_maximum_fusion.4), calls=%async_computation.1 | async-start | bytes 524288 | tf_op jit(solution)/shard_map/all_to_all | solution.py:37
Sparse Core Ops, SparseCore 0:
  13.7 81.2 all-reduce.2
where the time goes:
time: 148 us; the launch traced here: 147 us
  waiting for transfers between devices  98 us (66%)
  between operations  15.5 us (10%)
  starting transfers between devices  9.11 us (6%)
  local copies, waits for them, and re-layouts  8.73 us (6%)
  other arithmetic  8.24 us (6%)
  matrix products  7.31 us (5%)
    psum x1, waiting for transfers between devices, broadcast(): return lax.psum(block, axis)  80.7 us
    all_to_all x2, waiting for transfers between devices, regroup_apply(): lax.all_to_all(blocks, 'col', split_axis=1, concat_axis=1, tiled=True)  17.3 us
    all_to_all x2, starting transfers between devices, regroup_apply(): lax.all_to_all(blocks, 'col', split_axis=1, concat_axis=1, tiled=True)  9.11 us
    gather x2, local copies, waits for them, and re-layouts, worker(): jnp.take(piece.reshape(2, width, piece.shape[3]), mapping, axis=1)  4.23 us
    select_n x4, other arithmetic, worker(): jnp.take(piece.reshape(2, width, piece.shape[3]), mapping, axis=1)  3.52 us
  transfers between devices with their start and end apart: 3, of which 3 were waited for; matrix products, arithmetic and copies ran while one was open for 0% of the time, Pallas kernels for 0%

commit v1 on v0

v1 whole, which is shorter than its diff:
```python
import functools

import jax
import jax.numpy as jnp
from jax import lax
from jax.experimental import pallas as pl
from jax.experimental.pallas import tpu as pltpu
from jax.sharding import PartitionSpec as P

MESH = pl.DeviceIdType.MESH


def complex_product(first, second):
    real = jnp.dot(first[0], second[0], preferred_element_type=jnp.float32) - jnp.dot(
        first[1], second[1], preferred_element_type=jnp.float32
    )
    imaginary = jnp.dot(first[0], second[1], preferred_element_type=jnp.float32) + jnp.dot(
        first[1], second[0], preferred_element_type=jnp.float32
    )
    return jnp.stack([real, imaginary]).astype(jnp.bfloat16)


def fetch_branch(left_pool, right_pool, root, chosen):
    right_local = lax.dynamic_index_in_dim(right_pool[0], chosen, 0, keepdims=False)
    holder = lax.axis_index("row") == root
    local_branch = lax.cond(
        holder,
        lambda: complex_product(left_pool[0], right_local),
        lambda: jnp.zeros(left_pool[0].shape, jnp.bfloat16),
    )
    return lax.psum(local_branch, "row")


def plain_body(stem, left_pool, right_pool, owners, slices, relabels):
    count = owners.shape[0]
    branches = [fetch_branch(left_pool, right_pool, owners[k], slices[k]) for k in range(count)]
    state = complex_product(branches[0], stem)
    groups = lax.axis_size("col")
    _, width, open_size = state.shape
    for k in range(1, count):
        blocks = state.reshape(2, groups, width // groups, open_size)
        blocks = lax.all_to_all(blocks, "col", split_axis=1, concat_axis=1, tiled=True)
        state = jnp.take(blocks.reshape(2, width, open_size), relabels[k - 1], axis=1)
        state = complex_product(branches[k], state)
    return state


def step_order(n_col):
    return [(even, even + 1) for even in range(n_col - 2, -1, -2)]


def fused_kernel(
    n_row,
    n_col,
    owners_ref,
    slices_ref,
    relabels_ref,
    stem_hbm,
    left_hbm,
    right_hbm,
    out_ref,
    *scratch,
):
    branch = scratch[:n_col]
    (
        left_v,
        right_v,
        right_cat,
        state0,
        states,
        sends,
        local_sem,
        own_send,
        own_recv,
        far_send,
        far_recv,
        pass_send,
        pass_recv,
        side_send,
        swap_send,
        swap_recv,
    ) = scratch[n_col:]
    count = owners_ref.shape[0]
    width = left_v.shape[1]
    open_size = stem_hbm.shape[2]
    group = width // n_col
    row = lax.axis_index("row")
    col = lax.axis_index("col")

    def flip(index, bit):
        return index + bit - 2 * bit * (lax.rem(lax.div(index, bit), 2))

    def partner(step):
        other = col
        bit = 1
        while bit < n_col:
            if step & bit:
                other = flip(other, bit)
            bit *= 2
        return other

    partners = [partner(step) for step in range(n_col)]
    sibling = flip(row, 1)
    across = flip(row, 2)
    beside = partners[1]

    loads = [
        pltpu.make_async_copy(right_hbm.at[0], right_v, local_sem.at[0]),
        pltpu.make_async_copy(left_hbm.at[0], left_v, local_sem.at[1]),
        pltpu.make_async_copy(stem_hbm.at[0], state0.at[:, pl.ds(0, open_size)], local_sem.at[2]),
        pltpu.make_async_copy(
            stem_hbm.at[1], state0.at[:, pl.ds(open_size, open_size)], local_sem.at[3]
        ),
    ]
    for load in loads:
        load.start()

    barrier = pltpu.get_barrier_semaphore()
    greet = [(sibling, col), (across, col)] + [(row, other) for other in partners[1:]]
    for device in greet:
        pl.semaphore_signal(barrier, inc=1, device_id=device, device_id_type=MESH)

    chosen = slices_ref[0]
    wanted = lax.broadcasted_iota(jnp.int32, (1, width), 1)
    for k in range(1, count):
        mine = owners_ref[k] == row
        chosen = jnp.where(mine, slices_ref[k], chosen)
        mine_v = jnp.full((1, width), owners_ref[k], jnp.int32) == row
        wanted = jnp.where(mine_v, relabels_ref[k - 1 : k, :], wanted)
    places = lax.broadcasted_iota(jnp.int32, (width, width), 0)
    onehot = jnp.where(places == wanted, 1.0, 0.0).astype(jnp.bfloat16)
    loads[0].wait()
    for part in range(2):
        moved = lax.dot_general(
            right_v[chosen, part],
            onehot,
            (((1,), (1,)), ((), ())),
            preferred_element_type=jnp.float32,
        )
        right_cat[:, part * width : (part + 1) * width] = moved.astype(jnp.bfloat16)
    loads[1].wait()

    def rows_of(step):
        return pl.ds(pl.multiple_of(partners[step] * group, group), group)

    def copy(source, target, send, recv, device):
        return pltpu.make_async_remote_copy(
            src_ref=source,
            dst_ref=target,
            send_sem=send,
            recv_sem=recv,
            device_id=device,
            device_id_type=MESH,
        )

    def own_copy(step):
        slot = branch[step].at[row]
        return copy(slot, slot, own_send.at[step], own_recv.at[step], (sibling, col))

    def far_copy(step):
        slot = branch[step].at[row]
        return copy(slot, slot, far_send.at[step], far_recv.at[step], (across, col))

    def side_copy(step):
        return copy(
            branch[step].at[across],
            branch[step + 1].at[across],
            side_send.at[step],
            far_recv.at[step + 1],
            (row, beside),
        )

    def pass_copy(step):
        slot = branch[step].at[across]
        return copy(slot, slot, pass_send.at[step], pass_recv.at[step], (sibling, col))

    def swap_copy(turn, step):
        here = pl.ds(pl.multiple_of(col * group, group), group)
        return copy(
            sends.at[turn, step],
            states.at[turn, here, :],
            swap_send.at[turn, step],
            swap_recv.at[turn, step],
            (row, partners[step]),
        )

    def swap_arrival(turn, step):
        return copy(
            sends.at[turn, step],
            states.at[turn, rows_of(step), :],
            swap_send.at[turn, step],
            swap_recv.at[turn, step],
            (row, partners[step]),
        )

    def product(k, step, state):
        both = jnp.dot(branch[step][owners_ref[k]], state, preferred_element_type=jnp.float32)
        top, low = both[:group], both[group:]
        real = top[:, :open_size] - low[:, open_size:]
        imaginary = top[:, open_size:] + low[:, :open_size]
        return real.astype(jnp.bfloat16), imaginary.astype(jnp.bfloat16)

    def apply_and_send(k, step, state):
        turn = k
        real, imaginary = product(k, step, state)
        if step == 0:
            states[turn, rows_of(0), :open_size] = real
            states[turn, rows_of(0), open_size:] = imaginary
        else:
            sends[turn, step, :, :open_size] = real
            sends[turn, step, :, open_size:] = imaginary
            swap_copy(turn, step).start()

    order = step_order(n_col)
    started = False
    for pair in order:
        for step in pair:
            pieces = jnp.concatenate(
                [left_v[0, rows_of(step), :], left_v[1, rows_of(step), :]], axis=0
            )
            both = jnp.dot(pieces, right_cat[...], preferred_element_type=jnp.float32)
            top, low = both[:group], both[group:]
            branch[step][row, :group, :] = (top[:, :width] - low[:, width:]).astype(jnp.bfloat16)
            branch[step][row, group:, :] = (top[:, width:] + low[:, :width]).astype(jnp.bfloat16)
            if not started:
                pl.semaphore_wait(barrier, len(greet))
                started = True
            if step % 2 == 0:
                far_copy(step).start()
            own_copy(step).start()

    loads[2].wait()
    loads[3].wait()

    def finish_odd(step):
        far_copy(step).wait_recv()
        pass_copy(step).start()
        own_copy(step).wait_recv()
        pass_copy(step).wait_recv()
        apply_and_send(0, step, state0[...])

    late = None
    for even, odd in order:
        far_copy(even).wait_recv()
        side_copy(even).start()
        pass_copy(even).start()
        if late is not None:
            finish_odd(late)
        own_copy(even).wait_recv()
        pass_copy(even).wait_recv()
        apply_and_send(0, even, state0[...])
        late = odd
    finish_odd(late)

    for k in range(1, count):
        for step in range(1, n_col):
            swap_arrival(k - 1, step).wait_recv()
        for pair in order:
            for step in pair:
                if k < count - 1:
                    apply_and_send(k, step, states[k - 1])
                else:
                    real, imaginary = product(k, step, states[k - 1])
                    out_ref[0, rows_of(step), :] = real
                    out_ref[1, rows_of(step), :] = imaginary

    for step in range(n_col):
        own_copy(step).wait_send()
        pass_copy(step).wait_send()
        if step % 2 == 0:
            far_copy(step).wait_send()
            side_copy(step).wait_send()
        if step > 0:
            for turn in range(count - 1):
                swap_copy(turn, step).wait_send()


def fused_body(n_row, n_col, stem, left_pool, right_pool, owners, slices, relabels):
    count = owners.shape[0]
    _, width, open_size = stem.shape
    group = width // n_col
    dtype = stem.dtype
    dma = pltpu.SemaphoreType.DMA
    return pl.pallas_call(
        functools.partial(fused_kernel, n_row, n_col),
        out_shape=jax.ShapeDtypeStruct(stem.shape, dtype),
        in_specs=[
            pl.BlockSpec(memory_space=pltpu.SMEM),
            pl.BlockSpec(memory_space=pltpu.SMEM),
            pl.BlockSpec(memory_space=pltpu.VMEM),
            pl.BlockSpec(memory_space=pl.ANY),
            pl.BlockSpec(memory_space=pl.ANY),
            pl.BlockSpec(memory_space=pl.ANY),
        ],
        out_specs=pl.BlockSpec(memory_space=pltpu.VMEM),
        scratch_shapes=[pltpu.VMEM((n_row, 2 * group, width), dtype) for _ in range(n_col)]
        + [
            pltpu.VMEM(left_pool.shape[1:], dtype),
            pltpu.VMEM(right_pool.shape[1:], dtype),
            pltpu.VMEM((width, 2 * width), dtype),
            pltpu.VMEM((width, 2 * open_size), dtype),
            pltpu.VMEM((count - 1, width, 2 * open_size), dtype),
            pltpu.VMEM((count - 1, n_col, group, 2 * open_size), dtype),
            dma((4,)),
            dma((n_col,)),
            dma((n_col,)),
            dma((n_col,)),
            dma((n_col,)),
            dma((n_col,)),
            dma((n_col,)),
            dma((n_col,)),
            dma((count - 1, n_col)),
            dma((count - 1, n_col)),
        ],
        compiler_params=pltpu.CompilerParams(
            collective_id=0, has_side_effects=True, vmem_limit_bytes=40 * 1024 * 1024
        ),
        cost_estimate=pl.CostEstimate(
            flops=8 * width * width * (2 * width + count * open_size),
            bytes_accessed=2 * (left_pool.size + right_pool.size + 2 * stem.size),
            transcendentals=0,
        ),
    )(owners, slices, relabels, stem, left_pool, right_pool)


def solution(mesh):
    n_row, n_col = mesh.shape["row"], mesh.shape["col"]
    few = n_row == 4 and n_col >= 2 and n_col & (n_col - 1) == 0
    body = functools.partial(fused_body, n_row, n_col) if few else plain_body
    in_specs = (
        P(None, None, ("row", "col")),
        P("row", None, None, None),
        P("row", None, None, None, None),
        P(),
        P(),
        P(),
    )
    out_specs = P(None, None, ("row", "col"))
    return jax.shard_map(body, mesh=mesh, in_specs=in_specs, out_specs=out_specs, check_vma=False)
```

time: 148 us -> 46.5 us (0.31)
  waiting for transfers between devices: 98 us -> 0 us
  Pallas kernels: 0 us -> 39.7 us
  between operations: 15.5 us -> 0.02 us
  starting transfers between devices: 9.11 us -> 0 us
  other arithmetic: 8.24 us -> 0 us
  matrix products: 7.31 us -> 0 us
  local copies, waits for them, and re-layouts: 8.73 us -> 6.47 us
    psum x1 -> x0, waiting for transfers between devices: 80.7 us -> none  [broadcast(): return lax.psum(block, axis)]
    pallas_call x0 -> x1, Pallas kernels: none -> 39.7 us  [fused_body(): pl.pallas_call(functools.partial(fused_kernel, n_row, n_col), out_shape=j...]
    all_to_all x2 -> x0, waiting for transfers between devices: 17.3 us -> none  [regroup_apply(): lax.all_to_all(blocks, 'col', split_axis=1, concat_axis=1, tiled=True)]
    all_to_all x2 -> x0, starting transfers between devices: 9.11 us -> none  [regroup_apply(): lax.all_to_all(blocks, 'col', split_axis=1, concat_axis=1, tiled=True)]
    dot_general x12 -> x0, matrix products: 7.31 us -> none  [the longest x3 2.13 us: complex_product(): jnp.dot(first[0], second[0], preferred_element_type=jnp.float32)]
    select_n x6 -> x0, other arithmetic: 6.03 us -> none  [the longest x4 3.52 us: worker(): jnp.take(piece.reshape(2, width, piece.shape[3]), mapping, axis=1)]
    unnamed x12 -> x13, local copies, waits for them, and re-layouts: 1.63 us -> 6.47 us
    gather x2 -> x0, local copies, waits for them, and re-layouts: 4.23 us -> none  [worker(): jnp.take(piece.reshape(2, width, piece.shape[3]), mapping, axis=1)]
  transfers between devices with their start and end apart: 3 -> 0, of which waited for: 3 -> 0; matrix products, arithmetic and copies ran while one was open for 0% -> 0% of each run, Pallas kernels for 0% -> 0%
where the time goes in v1:
time: 46.5 us; the launch traced here: 46.2 us
  Pallas kernels  39.7 us (85%)
  local copies, waits for them, and re-layouts  6.47 us (14%)
    pallas_call x1, Pallas kernels, fused_body(): pl.pallas_call(functools.partial(fused_kernel, n_row, n_col), out_shape=j...  39.7 us
    unnamed x13, local copies, waits for them, and re-layouts  6.47 us

profile of v1, /device:TPU:0, one launch (start us, length us, event | category | flops | bytes accessed | tf_op | source)
XLA Modules:
  0.0 46.2 jit_solution(5826761307763512976)
XLA Ops:
  0.0 0.0 copy-start
  0.0 1.6 %copy-done = bf16[1,2,2,512,512]{4,3,2,1,0:T(8,128)(2,1)S(1)} copy-done((bf16[1,2,2,512,512]{4,3,2,1,0:T(8,128)(2,1)S(1)}, bf16[1,2,2,512,512]{4,3,2,1,0:T(8,128)(2,1)}, u32[]{:S(2)}) %copy-start) | copy-done | bytes 2097176
  1.6 0.0 copy-start.1
  1.6 1.2 %copy-done.1 = bf16[1,2,512,512]{3,2,1,0:T(8,128)(2,1)S(1)} copy-done((bf16[1,2,512,512]{3,2,1,0:T(8,128)(2,1)S(1)}, bf16[1,2,512,512]{3,2,1,0:T(8,128)(2,1)}, u32[]{:S(2)}) %copy-start.1) | copy-done | bytes 1048600
  2.8 0.0 copy-start.2
  2.8 0.9 %copy-done.2 = bf16[2,512,128]{2,1,0:T(8,128)(2,1)S(1)} copy-done((bf16[2,512,128]{2,1,0:T(8,128)(2,1)S(1)}, bf16[2,512,128]{2,1,0:T(8,128)(2,1)}, u32[]{:S(2)}) %copy-start.2) | copy-done | bytes 262168
  3.8 0.0 copy-start.3
  3.8 0.7 %copy-done.3 = s32[2,512]{1,0:T(2,128)S(1)} copy-done((s32[2,512]{1,0:T(2,128)S(1)}, s32[2,512]{1,0:T(2,128)}, u32[]{:S(2)}) %copy-start.3) | copy-done | bytes 4120
  4.5 0.0 copy-start.4
  4.5 0.7 %copy-done.4 = s32[3]{0:T(128)S(1)} copy-done((s32[3]{0:T(128)S(1)}, s32[3]{0:T(128)}, u32[]{:S(2)}) %copy-start.4) | copy-done | bytes 36
  5.1 0.0 copy-start.5
  5.1 0.7 %copy-done.5 = s32[3]{0:T(128)S(1)} copy-done((s32[3]{0:T(128)S(1)}, s32[3]{0:T(128)}, u32[]{:S(2)}) %copy-start.5) | copy-done | bytes 36
  5.8 39.7 %shard_map.64 = bf16[2,512,128]{2,1,0:T(8,128)(2,1)S(1)} custom-call(s32[3]{0:T(128)S(1)} %copy-done.4, s32[3]{0:T(128)S(1)} %copy-done.5, s32[2,512]{1,0:T(2,128)S(1)} %copy-done.3, bf16[2,512,128]{2,1,0:T(8,128)(2,1)S(1)} %copy-done.2, bf16[1,2,512,512]{3,2,1,0:T(8,128)(2,1)S(1)} %copy-done.1, bf16[1,2,2,512,512]{4,3,2,1,0:T(8,128)(2,1)S(1)} %copy-done), custom_call_target="tpu_custom_call" | custom-call | flops 2952790016 | bytes 3670016 | tf_op jit(solution)/shard_map/pallas_call | solution.py:284
  45.5 0.7 %copy.8 = bf16[2,512,128]{2,1,0:T(8,128)(2,1)} copy(bf16[2,512,128]{2,1,0:T(8,128)(2,1)S(1)} %shard_map.64) | data formatting | bytes 524288
Async XLA Ops:
  0.0 1.6 %copy-start = (bf16[1,2,2,512,512]{4,3,2,1,0:T(8,128)(2,1)S(1)}, bf16[1,2,2,512,512]{4,3,2,1,0:T(8,128)(2,1)}, u32[]{:S(2)}) copy-start(bf16[1,2,2,512,512]{4,3,2,1,0:T(8,128)(2,1)} %right_hbm.1) | copy-start | bytes 6291460
  1.6 1.2 %copy-start.1 = (bf16[1,2,512,512]{3,2,1,0:T(8,128)(2,1)S(1)}, bf16[1,2,512,512]{3,2,1,0:T(8,128)(2,1)}, u32[]{:S(2)}) copy-start(bf16[1,2,512,512]{3,2,1,0:T(8,128)(2,1)} %left_hbm.1) | copy-start | bytes 3145732
  2.8 0.9 %copy-start.2 = (bf16[2,512,128]{2,1,0:T(8,128)(2,1)S(1)}, bf16[2,512,128]{2,1,0:T(8,128)(2,1)}, u32[]{:S(2)}) copy-start(bf16[2,512,128]{2,1,0:T(8,128)(2,1)} %stem_hbm.1) | copy-start | bytes 786436
  3.8 0.7 %copy-start.3 = (s32[2,512]{1,0:T(2,128)S(1)}, s32[2,512]{1,0:T(2,128)}, u32[]{:S(2)}) copy-start(s32[2,512]{1,0:T(2,128)} %relabels_ref.1) | copy-start | bytes 12292
  4.5 0.7 %copy-start.4 = (s32[3]{0:T(128)S(1)}, s32[3]{0:T(128)}, u32[]{:S(2)}) copy-start(s32[3]{0:T(128)} %owners_ref.1) | copy-start | bytes 40
  5.1 0.7 %copy-start.5 = (s32[3]{0:T(128)S(1)}, s32[3]{0:T(128)}, u32[]{:S(2)}) copy-start(s32[3]{0:T(128)} %slices_ref.1) | copy-start | bytes 40

commit v2 on v1

--- a/solution.py
+++ b/solution.py
@@ -52,9 +52,9 @@
 def fused_kernel(
     n_row,
     n_col,
-    owners_ref,
-    slices_ref,
-    relabels_ref,
+    owners_hbm,
+    slices_hbm,
+    relabels_hbm,
     stem_hbm,
     left_hbm,
     right_hbm,
@@ -63,6 +63,9 @@
 ):
     branch = scratch[:n_col]
     (
+        owners_ref,
+        slices_ref,
+        relabels_ref,
         left_v,
         right_v,
         right_cat,
@@ -80,7 +83,7 @@
         swap_send,
         swap_recv,
     ) = scratch[n_col:]
-    count = owners_ref.shape[0]
+    count = owners_hbm.shape[0]
     width = left_v.shape[1]
     open_size = stem_hbm.shape[2]
     group = width // n_col
@@ -111,14 +114,18 @@
         pltpu.make_async_copy(
             stem_hbm.at[1], state0.at[:, pl.ds(open_size, open_size)], local_sem.at[3]
         ),
+        pltpu.make_async_copy(owners_hbm, owners_ref, local_sem.at[4]),
+        pltpu.make_async_copy(slices_hbm, slices_ref, local_sem.at[5]),
+        pltpu.make_async_copy(relabels_hbm, relabels_ref, local_sem.at[6]),
     ]
-    for load in loads:
-        load.start()
-
     barrier = pltpu.get_barrier_semaphore()
     greet = [(sibling, col), (across, col)] + [(row, other) for other in partners[1:]]
     for device in greet:
         pl.semaphore_signal(barrier, inc=1, device_id=device, device_id_type=MESH)
+    for place in (4, 5, 6, 0, 1, 2, 3):
+        loads[place].start()
+    for place in (4, 5, 6):
+        loads[place].wait()
 
     chosen = slices_ref[0]
     wanted = lax.broadcasted_iota(jnp.int32, (1, width), 1)
@@ -212,23 +219,20 @@
             swap_copy(turn, step).start()
 
     order = step_order(n_col)
-    started = False
-    for pair in order:
-        for step in pair:
-            pieces = jnp.concatenate(
-                [left_v[0, rows_of(step), :], left_v[1, rows_of(step), :]], axis=0
-            )
-            both = jnp.dot(pieces, right_cat[...], preferred_element_type=jnp.float32)
-            top, low = both[:group], both[group:]
-            branch[step][row, :group, :] = (top[:, :width] - low[:, width:]).astype(jnp.bfloat16)
-            branch[step][row, group:, :] = (top[:, width:] + low[:, :width]).astype(jnp.bfloat16)
-            if not started:
-                pl.semaphore_wait(barrier, len(greet))
-                started = True
-            if step % 2 == 0:
-                far_copy(step).start()
-            own_copy(step).start()
-
+
+    def make_own(step):
+        pieces = jnp.concatenate([left_v[0, rows_of(step), :], left_v[1, rows_of(step), :]], axis=0)
+        both = jnp.dot(pieces, right_cat[...], preferred_element_type=jnp.float32)
+        top, low = both[:group], both[group:]
+        branch[step][row, :group, :] = (top[:, :width] - low[:, width:]).astype(jnp.bfloat16)
+        branch[step][row, group:, :] = (top[:, width:] + low[:, :width]).astype(jnp.bfloat16)
+
+    for place, (even, _) in enumerate(order):
+        make_own(even)
+        if place == 0:
+            pl.semaphore_wait(barrier, len(greet))
+        far_copy(even).start()
+        own_copy(even).start()
     loads[2].wait()
     loads[3].wait()
 
@@ -244,6 +248,8 @@
         far_copy(even).wait_recv()
         side_copy(even).start()
         pass_copy(even).start()
+        make_own(odd)
+        own_copy(odd).start()
         if late is not None:
             finish_odd(late)
         own_copy(even).wait_recv()
@@ -285,23 +291,21 @@
         functools.partial(fused_kernel, n_row, n_col),
         out_shape=jax.ShapeDtypeStruct(stem.shape, dtype),
         in_specs=[
-            pl.BlockSpec(memory_space=pltpu.SMEM),
-            pl.BlockSpec(memory_space=pltpu.SMEM),
-            pl.BlockSpec(memory_space=pltpu.VMEM),
-            pl.BlockSpec(memory_space=pl.ANY),
-            pl.BlockSpec(memory_space=pl.ANY),
-            pl.BlockSpec(memory_space=pl.ANY),
+            pl.BlockSpec(memory_space=pl.ANY) for _ in range(6)
         ],
         out_specs=pl.BlockSpec(memory_space=pltpu.VMEM),
         scratch_shapes=[pltpu.VMEM((n_row, 2 * group, width), dtype) for _ in range(n_col)]
         + [
+            pltpu.SMEM(owners.shape, owners.dtype),
+            pltpu.SMEM(slices.shape, slices.dtype),
+            pltpu.VMEM(relabels.shape, relabels.dtype),
             pltpu.VMEM(left_pool.shape[1:], dtype),
             pltpu.VMEM(right_pool.shape[1:], dtype),
             pltpu.VMEM((width, 2 * width), dtype),
             pltpu.VMEM((width, 2 * open_size), dtype),
             pltpu.VMEM((count - 1, width, 2 * open_size), dtype),
             pltpu.VMEM((count - 1, n_col, group, 2 * open_size), dtype),
-            dma((4,)),
+            dma((7,)),
             dma((n_col,)),
             dma((n_col,)),
             dma((n_col,)),
@@ -313,7 +317,7 @@
             dma((count - 1, n_col)),
         ],
         compiler_params=pltpu.CompilerParams(
-            collective_id=0, has_side_effects=True, vmem_limit_bytes=40 * 1024 * 1024
+            collective_id=0, has_side_effects=True, vmem_limit_bytes=60 * 1024 * 1024
         ),
         cost_estimate=pl.CostEstimate(
             flops=8 * width * width * (2 * width + count * open_size),

time: 46.5 us -> 42.8 us (0.920)
  local copies, waits for them, and re-layouts: 6.47 us -> 1.67 us
  Pallas kernels: 39.7 us -> 41 us
    unnamed x13 -> x1, local copies, waits for them, and re-layouts: 6.47 us -> 1.67 us
    pallas_call x1, Pallas kernels: 39.7 us -> 41 us  [fused_body(): pl.pallas_call(functools.partial(fused_kernel, n_row, n_col), out_shape=j...]
where the time goes in v2:
time: 42.8 us; the launch traced here: 42.7 us
  Pallas kernels  41 us (96%)
  local copies, waits for them, and re-layouts  1.67 us (4%)
    pallas_call x1, Pallas kernels, fused_body(): pl.pallas_call(functools.partial(fused_kernel, n_row, n_col), out_shape=j...  41 us
    unnamed x1, local copies, waits for them, and re-layouts  1.67 us

profile of v2, /device:TPU:0, one launch (start us, length us, event | category | flops | bytes accessed | tf_op | source)
XLA Modules:
  0.0 42.7 jit_solution(6550265976619100216)
XLA Ops:
  0.0 41.0 %shard_map.64 = bf16[2,512,128]{2,1,0:T(8,128)(2,1)} custom-call(s32[3]{0:T(128)} %owners_hbm.1, s32[3]{0:T(128)} %slices_hbm.1, s32[2,512]{1,0:T(2,128)} %relabels_hbm.1, bf16[2,512,128]{2,1,0:T(8,128)(2,1)} %stem_hbm.1, bf16[1,2,512,512]{3,2,1,0:T(8,128)(2,1)} %left_hbm.1, bf16[1,2,2,512,512]{4,3,2,1,0:T(8,128)(2,1)} %right_hbm.1), custom_call_target="tpu_custom_call" | custom-call | flops 2952790016 | bytes 3670016 | tf_op jit(solution)/shard_map/pallas_call | solution.py:290
  41.0 1.7 %copy.8 = bf16[2,512,128]{2,1,0:T(8,128)(2,1)} copy(bf16[2,512,128]{2,1,0:T(8,128)(2,1)} %shard_map.64) | data formatting | bytes 524288

commit v3 on v2

v3 whole, which is shorter than its diff:
```python
import functools

import jax
import jax.numpy as jnp
from jax import lax
from jax.experimental import pallas as pl
from jax.experimental.pallas import tpu as pltpu
from jax.sharding import PartitionSpec as P

MESH = pl.DeviceIdType.MESH


def complex_product(first, second):
    real = jnp.dot(first[0], second[0], preferred_element_type=jnp.float32) - jnp.dot(
        first[1], second[1], preferred_element_type=jnp.float32
    )
    imaginary = jnp.dot(first[0], second[1], preferred_element_type=jnp.float32) + jnp.dot(
        first[1], second[0], preferred_element_type=jnp.float32
    )
    return jnp.stack([real, imaginary]).astype(jnp.bfloat16)


def fetch_branch(left_pool, right_pool, root, chosen):
    right_local = lax.dynamic_index_in_dim(right_pool[0], chosen, 0, keepdims=False)
    holder = lax.axis_index("row") == root
    local_branch = lax.cond(
        holder,
        lambda: complex_product(left_pool[0], right_local),
        lambda: jnp.zeros(left_pool[0].shape, jnp.bfloat16),
    )
    return lax.psum(local_branch, "row")


def plain_body(stem, left_pool, right_pool, owners, slices, relabels):
    count = owners.shape[0]
    branches = [fetch_branch(left_pool, right_pool, owners[k], slices[k]) for k in range(count)]
    state = complex_product(branches[0], stem)
    groups = lax.axis_size("col")
    _, width, open_size = state.shape
    for k in range(1, count):
        blocks = state.reshape(2, groups, width // groups, open_size)
        blocks = lax.all_to_all(blocks, "col", split_axis=1, concat_axis=1, tiled=True)
        state = jnp.take(blocks.reshape(2, width, open_size), relabels[k - 1], axis=1)
        state = complex_product(branches[k], state)
    return state


def flip(index, bit):
    return index + bit - 2 * bit * lax.rem(lax.div(index, bit), 2)


def fused_kernel(
    n_col,
    owners_hbm,
    slices_hbm,
    relabels_hbm,
    stem_hbm,
    left_hbm,
    right_hbm,
    out_ref,
    *scratch,
):
    pair = scratch[:n_col]
    slots = (scratch[n_col : 2 * n_col], scratch[2 * n_col : 3 * n_col])
    (
        owners_ref,
        slices_ref,
        relabels_ref,
        left_v,
        right_v,
        right_cat,
        state0,
        states,
        sends,
        local_sem,
        own_send,
        own_recv,
        far_send,
        far_recv,
        pass_send,
        pass_recv,
        side_send,
        swap_send,
        swap_recv,
    ) = scratch[3 * n_col :]
    count = owners_hbm.shape[0]
    width = left_v.shape[1]
    open_size = stem_hbm.shape[2]
    group = width // n_col
    row = lax.axis_index("row")
    col = lax.axis_index("col")
    core = lax.rem(row, 2)
    sibling = flip(row, 1)
    across = flip(row, 2)

    def at_distance(distance):
        other = col
        bit = 1
        while bit < n_col:
            if distance & bit:
                other = flip(other, bit)
            bit *= 2
        return other

    def partner(step):
        other = at_distance(step)
        return other + core * (flip(other, 2) - other)

    def distance(step):
        return step - 2 * core if step & 2 else step + 2 * core

    beside = at_distance(1)

    loads = [
        pltpu.make_async_copy(right_hbm.at[0], right_v, local_sem.at[0]),
        pltpu.make_async_copy(left_hbm.at[0], left_v, local_sem.at[1]),
        pltpu.make_async_copy(stem_hbm.at[0], state0.at[:, pl.ds(0, open_size)], local_sem.at[2]),
        pltpu.make_async_copy(
            stem_hbm.at[1], state0.at[:, pl.ds(open_size, open_size)], local_sem.at[3]
        ),
        pltpu.make_async_copy(owners_hbm, owners_ref, local_sem.at[4]),
        pltpu.make_async_copy(slices_hbm, slices_ref, local_sem.at[5]),
        pltpu.make_async_copy(relabels_hbm, relabels_ref, local_sem.at[6]),
    ]
    barrier = pltpu.get_barrier_semaphore()
    greet = [(sibling, col), (across, col)] + [(row, at_distance(d)) for d in range(1, n_col)]
    for device in greet:
        pl.semaphore_signal(barrier, inc=1, device_id=device, device_id_type=MESH)
    for place in (4, 5, 6, 0, 1, 2, 3):
        loads[place].start()
    for place in (4, 5, 6):
        loads[place].wait()

    chosen = slices_ref[0]
    wanted = lax.broadcasted_iota(jnp.int32, (1, width), 1)
    for k in range(1, count):
        mine = owners_ref[k] == row
        chosen = jnp.where(mine, slices_ref[k], chosen)
        mine_v = jnp.full((1, width), owners_ref[k], jnp.int32) == row
        wanted = jnp.where(mine_v, relabels_ref[k - 1 : k, :], wanted)
    places = lax.broadcasted_iota(jnp.int32, (width, width), 0)
    onehot = jnp.where(places == wanted, 1.0, 0.0).astype(jnp.bfloat16)
    loads[0].wait()
    for part in range(2):
        moved = lax.dot_general(
            right_v[chosen, part],
            onehot,
            (((1,), (1,)), ((), ())),
            preferred_element_type=jnp.float32,
        )
        right_cat[:, part * width : (part + 1) * width] = moved.astype(jnp.bfloat16)
    loads[1].wait()

    def use_of(holder):
        use = count
        for k in range(count - 1, -1, -1):
            use = jnp.where(owners_ref[k] == holder, k, use)
        return use

    def early_core(even_row):
        return jnp.where(use_of(even_row) < use_of(even_row + 1), 0, 1)

    my_even = row - core
    early_own = early_core(my_even)
    early_far = early_core(flip(my_even, 2))
    early_place = jnp.where(early_own == core, 0, 1)

    def rows_of(step):
        return pl.ds(pl.multiple_of(partner(step) * group, group), group)

    def copy(source, target, send, recv, device):
        return pltpu.make_async_remote_copy(
            src_ref=source,
            dst_ref=target,
            send_sem=send,
            recv_sem=recv,
            device_id=device,
            device_id_type=MESH,
        )

    def own_copy(step):
        to = step ^ 2
        return copy(
            pair[step].at[0], pair[to].at[1], own_send.at[step], own_recv.at[to], (sibling, col)
        )

    def own_arrival(step):
        return own_copy(step ^ 2)

    def far_copy(slot, step):
        return copy(
            slots[slot][step].at[0],
            slots[slot][step].at[1],
            far_send.at[slot, step],
            far_recv.at[slot, step],
            (across, col),
        )

    def side_copy(slot, step):
        to = step ^ 1
        return copy(
            slots[slot][step].at[1],
            slots[slot][to].at[1],
            side_send.at[slot, step],
            far_recv.at[slot, to],
            (row, beside),
        )

    def pass_copy(slot, step):
        to = step ^ 2
        return copy(
            slots[slot][step].at[1],
            slots[slot][to].at[1],
            pass_send.at[slot, step],
            pass_recv.at[slot, to],
            (sibling, col),
        )

    def pass_arrival(slot, step):
        return pass_copy(slot, step ^ 2)

    def swap_copy(turn, step):
        here = pl.ds(pl.multiple_of(col * group, group), group)
        apart = distance(step)
        return copy(
            sends.at[turn, step],
            states.at[turn, here, :],
            swap_send.at[turn, apart],
            swap_recv.at[turn, apart],
            (row, partner(step)),
        )

    def swap_any(turn, apart):
        other = at_distance(apart)
        there = pl.ds(pl.multiple_of(other * group, group), group)
        return copy(
            sends.at[turn, 0],
            states.at[turn, there, :],
            swap_send.at[turn, apart],
            swap_recv.at[turn, apart],
            (row, other),
        )

    def make_own(step):
        pieces = jnp.concatenate([left_v[0, rows_of(step), :], left_v[1, rows_of(step), :]], axis=0)
        both = jnp.dot(pieces, right_cat[...], preferred_element_type=jnp.float32)
        top, low = both[:group], both[group:]
        pair[step][0, :group, :] = (top[:, :width] - low[:, width:]).astype(jnp.bfloat16)
        pair[step][0, group:, :] = (top[:, width:] + low[:, :width]).astype(jnp.bfloat16)

    def place_own(step):
        own_arrival(step).wait_recv()
        slots[0][step][0] = pair[step][early_place]
        slots[1][step][0] = pair[step][1 - early_place]

    def branch_of(k, step):
        owner = owners_ref[k]
        far = jnp.where(owner - lax.rem(owner, 2) == my_even, 0, 1)
        early = slots[0][step][far]
        if k == 0:
            return early
        late = slots[1][step][far]
        first = jnp.where(far == 0, early_own, early_far)
        return jnp.where(lax.rem(owner, 2) == first, early, late)

    def product(k, step, state):
        both = jnp.dot(branch_of(k, step), state, preferred_element_type=jnp.float32)
        top, low = both[:group], both[group:]
        real = top[:, :open_size] - low[:, open_size:]
        imaginary = top[:, open_size:] + low[:, :open_size]
        return real.astype(jnp.bfloat16), imaginary.astype(jnp.bfloat16)

    def apply_and_send(k, step, state):
        real, imaginary = product(k, step, state)
        sends[k, step, :, :open_size] = real
        sends[k, step, :, open_size:] = imaginary
        if step in (0, 2):
            stays = core == step // 2

            @pl.when(stays)
            def _():
                states[k, rows_of(step), :open_size] = real
                states[k, rows_of(step), open_size:] = imaginary

            @pl.when(jnp.logical_not(stays))
            def _():
                swap_copy(k, step).start()
        else:
            swap_copy(k, step).start()

    bases = list(range(n_col - 4, -1, -4))
    direct = bases[: len(bases) // 2]
    shared = bases[len(bases) // 2 :]
    passes = [[], []]

    def forward(slot, step, side):
        far_copy(slot, step).wait_recv()
        if side:
            side_copy(slot, step).start()
        pass_copy(slot, step).start()
        passes[slot].append(step)

    for place, base in enumerate(bases):
        make_own(base + 2)
        if place == 0:
            pl.semaphore_wait(barrier, len(greet))
        own_copy(base + 2).start()
        make_own(base)
        own_copy(base).start()
        place_own(base)
        far_copy(0, base).start()
    loads[2].wait()
    loads[3].wait()
    for base in bases:
        for step in (base + 3, base + 1):
            make_own(step)
            own_copy(step).start()
    for base in bases:
        forward(0, base, True)
    for base in bases:
        for step in (base + 1, base + 2, base + 3):
            place_own(step)
    late_far = shared + [step for base in direct for step in (base, base + 1)]
    far_copy(0, bases[-1]).wait_send()
    for step in late_far:
        far_copy(1, step).start()

    for base in bases:
        apply_and_send(0, base, state0[...])
        pass_arrival(0, base + 2).wait_recv()
        apply_and_send(0, base + 2, state0[...])
    for base in bases:
        forward(0, base + 1, False)
        apply_and_send(0, base + 1, state0[...])
        pass_arrival(0, base + 3).wait_recv()
        apply_and_send(0, base + 3, state0[...])

    for base in shared:
        forward(1, base, True)
    for apart in range(1, n_col):
        swap_any(0, apart).wait_recv()

    def apply_late(k, step):
        apply_and_send(k, step, states[k - 1])

    for base in shared:
        pass_arrival(1, base + 2).wait_recv()
        apply_late(1, base)
        apply_late(1, base + 2)
    for base in direct:
        for step in (base, base + 1):
            forward(1, step, False)
            apply_late(1, step)
            pass_arrival(1, step + 2).wait_recv()
            apply_late(1, step + 2)
    for base in shared:
        forward(1, base + 1, False)
        apply_late(1, base + 1)
        pass_arrival(1, base + 3).wait_recv()
        apply_late(1, base + 3)

    for k in range(2, count):
        for apart in range(1, n_col):
            swap_any(k - 1, apart).wait_recv()
        for step in range(n_col):
            if k < count - 1:
                apply_late(k, step)
            else:
                real, imaginary = product(k, step, states[k - 1])
                out_ref[0, rows_of(step), :] = real
                out_ref[1, rows_of(step), :] = imaginary

    for step in range(n_col):
        own_copy(step).wait_send()
    for base in bases[:-1]:
        far_copy(0, base).wait_send()
    for base in bases:
        side_copy(0, base).wait_send()
    for step in late_far:
        far_copy(1, step).wait_send()
    for base in shared:
        side_copy(1, base).wait_send()
    for slot in range(2):
        for step in passes[slot]:
            pass_copy(slot, step).wait_send()
    for turn in range(count - 1):
        for apart in range(1, n_col):
            swap_any(turn, apart).wait_send()


def fused_body(n_col, stem, left_pool, right_pool, owners, slices, relabels):
    count = owners.shape[0]
    _, width, open_size = stem.shape
    group = width // n_col
    dtype = stem.dtype
    dma = pltpu.SemaphoreType.DMA
    return pl.pallas_call(
        functools.partial(fused_kernel, n_col),
        out_shape=jax.ShapeDtypeStruct(stem.shape, dtype),
        in_specs=[
            pl.BlockSpec(memory_space=pl.ANY) for _ in range(6)
        ],
        out_specs=pl.BlockSpec(memory_space=pltpu.VMEM),
        scratch_shapes=[pltpu.VMEM((2, 2 * group, width), dtype) for _ in range(3 * n_col)]
        + [
            pltpu.SMEM(owners.shape, owners.dtype),
            pltpu.SMEM(slices.shape, slices.dtype),
            pltpu.VMEM(relabels.shape, relabels.dtype),
            pltpu.VMEM(left_pool.shape[1:], dtype),
            pltpu.VMEM(right_pool.shape[1:], dtype),
            pltpu.VMEM((width, 2 * width), dtype),
            pltpu.VMEM((width, 2 * open_size), dtype),
            pltpu.VMEM((count - 1, width, 2 * open_size), dtype),
            pltpu.VMEM((count - 1, n_col, group, 2 * open_size), dtype),
            dma((7,)),
            dma((n_col,)),
            dma((n_col,)),
            dma((2, n_col)),
            dma((2, n_col)),
            dma((2, n_col)),
            dma((2, n_col)),
            dma((2, n_col)),
            dma((count - 1, n_col)),
            dma((count - 1, n_col)),
        ],
        compiler_params=pltpu.CompilerParams(
            collective_id=0, has_side_effects=True, vmem_limit_bytes=60 * 1024 * 1024
        ),
        cost_estimate=pl.CostEstimate(
            flops=8 * width * width * (2 * width + count * open_size),
            bytes_accessed=2 * (left_pool.size + right_pool.size + 2 * stem.size),
            transcendentals=0,
        ),
    )(owners, slices, relabels, stem, left_pool, right_pool)


def solution(mesh):
    n_row, n_col = mesh.shape["row"], mesh.shape["col"]
    few = n_row == 4 and n_col >= 4 and n_col & (n_col - 1) == 0
    body = functools.partial(fused_body, n_col) if few else plain_body
    in_specs = (
        P(None, None, ("row", "col")),
        P("row", None, None, None),
        P("row", None, None, None, None),
        P(),
        P(),
        P(),
    )
    out_specs = P(None, None, ("row", "col"))
    return jax.shard_map(body, mesh=mesh, in_specs=in_specs, out_specs=out_specs, check_vma=False)
```

time: 42.8 us -> 37.5 us (0.88)
  Pallas kernels: 41 us -> 35.6 us
    pallas_call x1, Pallas kernels: 41 us -> 35.6 us  [fused_body(): pl.pallas_call(functools.partial(fused_kernel, n_col), out_shape=jax.Shap...]
where the time goes in v3:
time: 37.5 us; the launch traced here: 37.3 us
  Pallas kernels  35.6 us (95%)
  local copies, waits for them, and re-layouts  1.67 us (4%)
    pallas_call x1, Pallas kernels, fused_body(): pl.pallas_call(functools.partial(fused_kernel, n_col), out_shape=jax.Shap...  35.6 us
    unnamed x1, local copies, waits for them, and re-layouts  1.67 us

profile of v3, /device:TPU:0, one launch (start us, length us, event | category | flops | bytes accessed | tf_op | source)
XLA Modules:
  0.0 37.3 jit_solution(882691676687344559)
XLA Ops:
  0.0 35.6 %shard_map.64 = bf16[2,512,128]{2,1,0:T(8,128)(2,1)} custom-call(s32[3]{0:T(128)} %owners_hbm.1, s32[3]{0:T(128)} %slices_hbm.1, s32[2,512]{1,0:T(2,128)} %relabels_hbm.1, bf16[2,512,128]{2,1,0:T(8,128)(2,1)} %stem_hbm.1, bf16[1,2,512,512]{3,2,1,0:T(8,128)(2,1)} %left_hbm.1, bf16[1,2,2,512,512]{4,3,2,1,0:T(8,128)(2,1)} %right_hbm.1), custom_call_target="tpu_custom_call" | custom-call | flops 2952790016 | bytes 3670016 | tf_op jit(solution)/shard_map/pallas_call | solution.py:397
  35.6 1.7 %copy.8 = bf16[2,512,128]{2,1,0:T(8,128)(2,1)} copy(bf16[2,512,128]{2,1,0:T(8,128)(2,1)} %shard_map.64) | data formatting | bytes 524288

commit v4 on v3

--- a/solution.py
+++ b/solution.py
@@ -68,7 +68,8 @@
         relabels_ref,
         left_v,
         right_v,
-        right_cat,
+        onehot_v,
+        last_v,
         state0,
         states,
         sends,
@@ -139,16 +140,8 @@
         mine_v = jnp.full((1, width), owners_ref[k], jnp.int32) == row
         wanted = jnp.where(mine_v, relabels_ref[k - 1 : k, :], wanted)
     places = lax.broadcasted_iota(jnp.int32, (width, width), 0)
-    onehot = jnp.where(places == wanted, 1.0, 0.0).astype(jnp.bfloat16)
+    onehot_v[...] = jnp.where(places == wanted, 1.0, 0.0).astype(jnp.bfloat16)
     loads[0].wait()
-    for part in range(2):
-        moved = lax.dot_general(
-            right_v[chosen, part],
-            onehot,
-            (((1,), (1,)), ((), ())),
-            preferred_element_type=jnp.float32,
-        )
-        right_cat[:, part * width : (part + 1) * width] = moved.astype(jnp.bfloat16)
     loads[1].wait()
 
     def use_of(holder):
@@ -187,37 +180,37 @@
     def own_arrival(step):
         return own_copy(step ^ 2)
 
-    def far_copy(slot, step):
+    def far_copy(slot, step, part):
+        rows = pl.ds(part * group, group)
         return copy(
-            slots[slot][step].at[0],
-            slots[slot][step].at[1],
-            far_send.at[slot, step],
-            far_recv.at[slot, step],
+            slots[slot][step].at[0, rows],
+            slots[slot][step].at[1, rows],
+            far_send.at[slot, step, part],
+            far_recv.at[slot, step, part],
             (across, col),
         )
 
-    def side_copy(slot, step):
+    def side_copy(slot, step, part):
         to = step ^ 1
+        rows = pl.ds(part * group, group)
         return copy(
-            slots[slot][step].at[1],
-            slots[slot][to].at[1],
-            side_send.at[slot, step],
-            far_recv.at[slot, to],
+            slots[slot][step].at[1, rows],
+            slots[slot][to].at[1, rows],
+            side_send.at[slot, step, part],
+            far_recv.at[slot, to, part],
             (row, beside),
         )
 
-    def pass_copy(slot, step):
+    def pass_copy(slot, step, part):
         to = step ^ 2
+        rows = pl.ds(part * group, group)
         return copy(
-            slots[slot][step].at[1],
-            slots[slot][to].at[1],
-            pass_send.at[slot, step],
-            pass_recv.at[slot, to],
+            slots[slot][step].at[1, rows],
+            slots[slot][to].at[1, rows],
+            pass_send.at[slot, step, part],
+            pass_recv.at[slot, to, part],
             (sibling, col),
         )
-
-    def pass_arrival(slot, step):
-        return pass_copy(slot, step ^ 2)
 
     def swap_copy(turn, step):
         here = pl.ds(pl.multiple_of(col * group, group), group)
@@ -241,12 +234,25 @@
             (row, other),
         )
 
-    def make_own(step):
-        pieces = jnp.concatenate([left_v[0, rows_of(step), :], left_v[1, rows_of(step), :]], axis=0)
-        both = jnp.dot(pieces, right_cat[...], preferred_element_type=jnp.float32)
-        top, low = both[:group], both[group:]
-        pair[step][0, :group, :] = (top[:, :width] - low[:, width:]).astype(jnp.bfloat16)
-        pair[step][0, group:, :] = (top[:, width:] + low[:, :width]).astype(jnp.bfloat16)
+    def make_own(first, second):
+        pieces = jnp.concatenate(
+            [left_v[part, rows_of(step), :] for step in (first, second) for part in range(2)], axis=0
+        )
+        by_real = jnp.dot(pieces, right_v[chosen, 0], preferred_element_type=jnp.float32)
+        by_imag = jnp.dot(pieces, right_v[chosen, 1], preferred_element_type=jnp.float32)
+        rows = []
+        for start in (0, 2 * group):
+            middle, stop = start + group, start + 2 * group
+            rows.append(by_real[start:middle] - by_imag[middle:stop])
+            rows.append(by_imag[start:middle] + by_real[middle:stop])
+        moved = lax.dot_general(
+            jnp.concatenate(rows, axis=0).astype(jnp.bfloat16),
+            onehot_v[...],
+            (((1,), (1,)), ((), ())),
+            preferred_element_type=jnp.float32,
+        ).astype(jnp.bfloat16)
+        pair[first][0] = moved[: 2 * group]
+        pair[second][0] = moved[2 * group :]
 
     def place_own(step):
         own_arrival(step).wait_recv()
@@ -264,14 +270,18 @@
         return jnp.where(lax.rem(owner, 2) == first, early, late)
 
     def product(k, step, state):
-        both = jnp.dot(branch_of(k, step), state, preferred_element_type=jnp.float32)
+        return parts_of(jnp.dot(branch_of(k, step), state, preferred_element_type=jnp.float32))
+
+    def parts_of(both):
         top, low = both[:group], both[group:]
         real = top[:, :open_size] - low[:, open_size:]
         imaginary = top[:, open_size:] + low[:, :open_size]
         return real.astype(jnp.bfloat16), imaginary.astype(jnp.bfloat16)
 
     def apply_and_send(k, step, state):
-        real, imaginary = product(k, step, state)
+        send_on(k, step, *product(k, step, state))
+
+    def send_on(k, step, real, imaginary):
         sends[k, step, :, :open_size] = real
         sends[k, step, :, open_size:] = imaginary
         if step in (0, 2):
@@ -291,52 +301,88 @@
     bases = list(range(n_col - 4, -1, -4))
     direct = bases[: len(bases) // 2]
     shared = bases[len(bases) // 2 :]
-    passes = [[], []]
-
-    def forward(slot, step, side):
-        far_copy(slot, step).wait_recv()
-        if side:
-            side_copy(slot, step).start()
-        pass_copy(slot, step).start()
-        passes[slot].append(step)
+    late_far = shared + [step for base in direct for step in (base, base + 1)]
+    halves = range(2)
+    journey = [(0, base, part) for base in bases for part in halves]
+    journey += [(1, step, part) for step in late_far for part in halves]
+    window = 3
+    sided = {(0, base) for base in bases} | {(1, base) for base in shared}
+    passes = []
+
+    def hand_on(slot, step, part):
+        pass_copy(slot, step, part).start()
+        passes.append((slot, step, part))
+
+    def advance(number):
+        slot, step, part = journey[number]
+        far_copy(slot, step, part).wait_recv()
+        if (slot, step) in sided:
+            side_copy(slot, step, part).start()
+        hand_on(slot, step, part)
+        far_copy(slot, step, part).wait_send()
+        if number + window < len(journey):
+            far_copy(*journey[number + window]).start()
+
+    def from_beside(slot, step):
+        for part in halves:
+            far_copy(slot, step, part).wait_recv()
+            hand_on(slot, step, part)
+
+    def from_sibling(slot, step):
+        for part in halves:
+            pass_copy(slot, step ^ 2, part).wait_recv()
 
     for place, base in enumerate(bases):
-        make_own(base + 2)
+        make_own(base + 2, base)
         if place == 0:
             pl.semaphore_wait(barrier, len(greet))
         own_copy(base + 2).start()
-        make_own(base)
         own_copy(base).start()
+    begun = 0
+    for base in bases:
         place_own(base)
-        far_copy(0, base).start()
+        while begun < window and journey[begun][:2] == (0, base):
+            far_copy(*journey[begun]).start()
+            begun += 1
     loads[2].wait()
     loads[3].wait()
-    for base in bases:
-        for step in (base + 3, base + 1):
-            make_own(step)
-            own_copy(step).start()
-    for base in bases:
-        forward(0, base, True)
-    for base in bases:
-        for step in (base + 1, base + 2, base + 3):
+    odd_left = list(bases)
+
+    def make_odd():
+        if odd_left:
+            base = odd_left.pop(0)
+            make_own(base + 3, base + 1)
+            own_copy(base + 3).start()
+            own_copy(base + 1).start()
+
+    make_odd()
+    arrived = 0
+    advance(0)
+    while odd_left:
+        make_odd()
+    advance(1)
+    arrived = 2
+    for step in range(n_col):
+        if step not in bases:
             place_own(step)
-    late_far = shared + [step for base in direct for step in (base, base + 1)]
-    far_copy(0, bases[-1]).wait_send()
-    for step in late_far:
-        far_copy(1, step).start()
-
-    for base in bases:
+    for place, base in enumerate(bases):
+        if place > 0:
+            for part in halves:
+                advance(arrived)
+                arrived += 1
         apply_and_send(0, base, state0[...])
-        pass_arrival(0, base + 2).wait_recv()
+        from_sibling(0, base + 2)
         apply_and_send(0, base + 2, state0[...])
-    for base in bases:
-        forward(0, base + 1, False)
+    for place, base in enumerate(bases):
+        from_beside(0, base + 1)
         apply_and_send(0, base + 1, state0[...])
-        pass_arrival(0, base + 3).wait_recv()
+        from_sibling(0, base + 3)
         apply_and_send(0, base + 3, state0[...])
-
-    for base in shared:
-        forward(1, base, True)
+        if place < len(shared):
+            for part in halves:
+                advance(arrived)
+                arrived += 1
+
     for apart in range(1, n_col):
         swap_any(0, apart).wait_recv()
 
@@ -344,45 +390,52 @@
         apply_and_send(k, step, states[k - 1])
 
     for base in shared:
-        pass_arrival(1, base + 2).wait_recv()
+        from_sibling(1, base + 2)
         apply_late(1, base)
         apply_late(1, base + 2)
+    waiting = list(shared)
+
+    def finish_shared():
+        if waiting:
+            base = waiting.pop(0)
+            from_beside(1, base + 1)
+            apply_late(1, base + 1)
+            from_sibling(1, base + 3)
+            apply_late(1, base + 3)
+
     for base in direct:
         for step in (base, base + 1):
-            forward(1, step, False)
+            for part in halves:
+                advance(arrived)
+                arrived += 1
             apply_late(1, step)
-            pass_arrival(1, step + 2).wait_recv()
+            from_sibling(1, step + 2)
             apply_late(1, step + 2)
-    for base in shared:
-        forward(1, base + 1, False)
-        apply_late(1, base + 1)
-        pass_arrival(1, base + 3).wait_recv()
-        apply_late(1, base + 3)
+            finish_shared()
+    while waiting:
+        finish_shared()
 
     for k in range(2, count):
+        for step in range(n_col):
+            last_v[step * 2 * group : (step + 1) * 2 * group, :] = branch_of(k, step)
         for apart in range(1, n_col):
             swap_any(k - 1, apart).wait_recv()
+        both = jnp.dot(last_v[...], states[k - 1], preferred_element_type=jnp.float32)
         for step in range(n_col):
+            real, imaginary = parts_of(both[step * 2 * group : (step + 1) * 2 * group])
             if k < count - 1:
-                apply_late(k, step)
+                send_on(k, step, real, imaginary)
             else:
-                real, imaginary = product(k, step, states[k - 1])
                 out_ref[0, rows_of(step), :] = real
                 out_ref[1, rows_of(step), :] = imaginary
 
     for step in range(n_col):
         own_copy(step).wait_send()
-    for base in bases[:-1]:
-        far_copy(0, base).wait_send()
-    for base in bases:
-        side_copy(0, base).wait_send()
-    for step in late_far:
-        far_copy(1, step).wait_send()
-    for base in shared:
-        side_copy(1, base).wait_send()
-    for slot in range(2):
-        for step in passes[slot]:
-            pass_copy(slot, step).wait_send()
+    for slot, step in sorted(sided):
+        for part in halves:
+            side_copy(slot, step, part).wait_send()
+    for slot, step, part in passes:
+        pass_copy(slot, step, part).wait_send()
     for turn in range(count - 1):
         for apart in range(1, n_col):
             swap_any(turn, apart).wait_send()
@@ -408,18 +461,19 @@
             pltpu.VMEM(relabels.shape, relabels.dtype),
             pltpu.VMEM(left_pool.shape[1:], dtype),
             pltpu.VMEM(right_pool.shape[1:], dtype),
-            pltpu.VMEM((width, 2 * width), dtype),
+            pltpu.VMEM((width, width), dtype),
+            pltpu.VMEM((2 * width, width), dtype),
             pltpu.VMEM((width, 2 * open_size), dtype),
             pltpu.VMEM((count - 1, width, 2 * open_size), dtype),
             pltpu.VMEM((count - 1, n_col, group, 2 * open_size), dtype),
             dma((7,)),
             dma((n_col,)),
             dma((n_col,)),
-            dma((2, n_col)),
-            dma((2, n_col)),
-            dma((2, n_col)),
-            dma((2, n_col)),
-            dma((2, n_col)),
+            dma((2, n_col, 2)),
+            dma((2, n_col, 2)),
+            dma((2, n_col, 2)),
+            dma((2, n_col, 2)),
+            dma((2, n_col, 2)),
             dma((count - 1, n_col)),
             dma((count - 1, n_col)),
         ],

time: 37.5 us -> 38.6 us (1.029)
  Pallas kernels: 35.6 us -> 36.8 us
    pallas_call x1, Pallas kernels: 35.6 us -> 36.8 us  [fused_body(): pl.pallas_call(functools.partial(fused_kernel, n_col), out_shape=jax.Shap...]
where the time goes in v4:
time: 38.6 us; the launch traced here: 38.5 us
  Pallas kernels  36.8 us (95%)
  local copies, waits for them, and re-layouts  1.67 us (4%)
    pallas_call x1, Pallas kernels, fused_body(): pl.pallas_call(functools.partial(fused_kernel, n_col), out_shape=jax.Shap...  36.8 us
    unnamed x1, local copies, waits for them, and re-layouts  1.67 us

profile of v4, /device:TPU:0, one launch (start us, length us, event | category | flops | bytes accessed | tf_op | source)
XLA Modules:
  0.0 38.5 jit_solution(1765643047439777124)
XLA Ops:
  0.0 36.8 %shard_map.64 = bf16[2,512,128]{2,1,0:T(8,128)(2,1)} custom-call(s32[3]{0:T(128)} %owners_hbm.1, s32[3]{0:T(128)} %slices_hbm.1, s32[2,512]{1,0:T(2,128)} %relabels_hbm.1, bf16[2,512,128]{2,1,0:T(8,128)(2,1)} %stem_hbm.1, bf16[1,2,512,512]{3,2,1,0:T(8,128)(2,1)} %left_hbm.1, bf16[1,2,2,512,512]{4,3,2,1,0:T(8,128)(2,1)} %right_hbm.1), custom_call_target="tpu_custom_call" | custom-call | flops 2952790016 | bytes 3670016 | tf_op jit(solution)/shard_map/pallas_call | solution.py:450
  36.8 1.7 %copy.8 = bf16[2,512,128]{2,1,0:T(8,128)(2,1)} copy(bf16[2,512,128]{2,1,0:T(8,128)(2,1)} %shard_map.64) | data formatting | bytes 524288

commit v5 on v4

--- a/solution.py
+++ b/solution.py
@@ -299,13 +299,13 @@
             swap_copy(k, step).start()
 
     bases = list(range(n_col - 4, -1, -4))
-    direct = bases[: len(bases) // 2]
-    shared = bases[len(bases) // 2 :]
+    shared = bases[: -(len(bases) // 2) or None]
+    direct = bases[len(shared) :]
     late_far = shared + [step for base in direct for step in (base, base + 1)]
     halves = range(2)
     journey = [(0, base, part) for base in bases for part in halves]
     journey += [(1, step, part) for step in late_far for part in halves]
-    window = 3
+    early_halves = 2 * len(bases)
     sided = {(0, base) for base in bases} | {(1, base) for base in shared}
     passes = []
 
@@ -320,8 +320,9 @@
             side_copy(slot, step, part).start()
         hand_on(slot, step, part)
         far_copy(slot, step, part).wait_send()
-        if number + window < len(journey):
-            far_copy(*journey[number + window]).start()
+        if number == early_halves - 2:
+            for later in journey[early_halves:]:
+                far_copy(*later).start()
 
     def from_beside(slot, step):
         for part in halves:
@@ -338,12 +339,10 @@
             pl.semaphore_wait(barrier, len(greet))
         own_copy(base + 2).start()
         own_copy(base).start()
-    begun = 0
     for base in bases:
         place_own(base)
-        while begun < window and journey[begun][:2] == (0, base):
-            far_copy(*journey[begun]).start()
-            begun += 1
+        for part in halves:
+            far_copy(0, base, part).start()
     loads[2].wait()
     loads[3].wait()
     odd_left = list(bases)

time: 38.6 us -> 37.6 us (0.974)
  Pallas kernels: 36.8 us -> 35.8 us
    pallas_call x1, Pallas kernels: 36.8 us -> 35.8 us  [fused_body(): pl.pallas_call(functools.partial(fused_kernel, n_col), out_shape=jax.Shap...]
where the time goes in v5:
time: 37.6 us; the launch traced here: 37.4 us
  Pallas kernels  35.8 us (95%)
  local copies, waits for them, and re-layouts  1.67 us (4%)
    pallas_call x1, Pallas kernels, fused_body(): pl.pallas_call(functools.partial(fused_kernel, n_col), out_shape=jax.Shap...  35.8 us
    unnamed x1, local copies, waits for them, and re-layouts  1.67 us

profile of v5, /device:TPU:0, one launch (start us, length us, event | category | flops | bytes accessed | tf_op | source)
XLA Modules:
  0.0 37.4 jit_solution(16237921931259204558)
XLA Ops:
  0.0 35.8 %shard_map.64 = bf16[2,512,128]{2,1,0:T(8,128)(2,1)} custom-call(s32[3]{0:T(128)} %owners_hbm.1, s32[3]{0:T(128)} %slices_hbm.1, s32[2,512]{1,0:T(2,128)} %relabels_hbm.1, bf16[2,512,128]{2,1,0:T(8,128)(2,1)} %stem_hbm.1, bf16[1,2,512,512]{3,2,1,0:T(8,128)(2,1)} %left_hbm.1, bf16[1,2,2,512,512]{4,3,2,1,0:T(8,128)(2,1)} %right_hbm.1), custom_call_target="tpu_custom_call" | custom-call | flops 2952790016 | bytes 3670016 | tf_op jit(solution)/shard_map/pallas_call | solution.py:449
  35.8 1.7 %copy.8 = bf16[2,512,128]{2,1,0:T(8,128)(2,1)} copy(bf16[2,512,128]{2,1,0:T(8,128)(2,1)} %shard_map.64) | data formatting | bytes 524288

commit v6 on v5

--- a/solution.py
+++ b/solution.py
@@ -299,7 +299,7 @@
             swap_copy(k, step).start()
 
     bases = list(range(n_col - 4, -1, -4))
-    shared = bases[: -(len(bases) // 2) or None]
+    shared = bases
     direct = bases[len(shared) :]
     late_far = shared + [step for base in direct for step in (base, base + 1)]
     halves = range(2)

time: 37.6 us -> 37.8 us (level)
  no operation moved by 1% of the time
where the time goes in v6:
time: 37.8 us; the launch traced here: 37.7 us
  Pallas kernels  36 us (95%)
  local copies, waits for them, and re-layouts  1.67 us (4%)
    pallas_call x1, Pallas kernels, fused_body(): pl.pallas_call(functools.partial(fused_kernel, n_col), out_shape=jax.Shap...  36 us
    unnamed x1, local copies, waits for them, and re-layouts  1.67 us

profile of v6, /device:TPU:0, one launch (start us, length us, event | category | flops | bytes accessed | tf_op | source)
XLA Modules:
  0.0 37.7 jit_solution(2606511390473361292)
XLA Ops:
  0.0 36.0 %shard_map.64 = bf16[2,512,128]{2,1,0:T(8,128)(2,1)} custom-call(s32[3]{0:T(128)} %owners_hbm.1, s32[3]{0:T(128)} %slices_hbm.1, s32[2,512]{1,0:T(2,128)} %relabels_hbm.1, bf16[2,512,128]{2,1,0:T(8,128)(2,1)} %stem_hbm.1, bf16[1,2,512,512]{3,2,1,0:T(8,128)(2,1)} %left_hbm.1, bf16[1,2,2,512,512]{4,3,2,1,0:T(8,128)(2,1)} %right_hbm.1), custom_call_target="tpu_custom_call" | custom-call | flops 2952790016 | bytes 3670016 | tf_op jit(solution)/shard_map/pallas_call | solution.py:449
  36.0 1.7 %copy.8 = bf16[2,512,128]{2,1,0:T(8,128)(2,1)} copy(bf16[2,512,128]{2,1,0:T(8,128)(2,1)} %shard_map.64) | data formatting | bytes 524288

commit v7 on v5

--- a/solution.py
+++ b/solution.py
@@ -8,6 +8,7 @@
 from jax.sharding import PartitionSpec as P
 
 MESH = pl.DeviceIdType.MESH
+PARTS = 1
 
 
 def complex_product(first, second):
@@ -112,25 +113,33 @@
 
     beside = at_distance(1)
 
+    places = [
+        (owners_hbm, owners_ref),
+        (slices_hbm, slices_ref),
+        (relabels_hbm, relabels_ref),
+    ]
+    small = len(places)
+    for value in range(right_v.shape[0]):
+        for part in range(2):
+            places.append((right_hbm.at[0, value, part], right_v.at[value, part]))
+    for part in range(2):
+        places.append((left_hbm.at[0, part], left_v.at[part]))
+    pools = len(places)
+    for part in range(2):
+        lanes = pl.ds(part * open_size, open_size)
+        places.append((stem_hbm.at[part], state0.at[:, lanes]))
     loads = [
-        pltpu.make_async_copy(right_hbm.at[0], right_v, local_sem.at[0]),
-        pltpu.make_async_copy(left_hbm.at[0], left_v, local_sem.at[1]),
-        pltpu.make_async_copy(stem_hbm.at[0], state0.at[:, pl.ds(0, open_size)], local_sem.at[2]),
-        pltpu.make_async_copy(
-            stem_hbm.at[1], state0.at[:, pl.ds(open_size, open_size)], local_sem.at[3]
-        ),
-        pltpu.make_async_copy(owners_hbm, owners_ref, local_sem.at[4]),
-        pltpu.make_async_copy(slices_hbm, slices_ref, local_sem.at[5]),
-        pltpu.make_async_copy(relabels_hbm, relabels_ref, local_sem.at[6]),
+        pltpu.make_async_copy(source, target, local_sem.at[number])
+        for number, (source, target) in enumerate(places)
     ]
     barrier = pltpu.get_barrier_semaphore()
     greet = [(sibling, col), (across, col)] + [(row, at_distance(d)) for d in range(1, n_col)]
     for device in greet:
         pl.semaphore_signal(barrier, inc=1, device_id=device, device_id_type=MESH)
-    for place in (4, 5, 6, 0, 1, 2, 3):
-        loads[place].start()
-    for place in (4, 5, 6):
-        loads[place].wait()
+    for load in loads:
+        load.start()
+    for load in loads[:small]:
+        load.wait()
 
     chosen = slices_ref[0]
     wanted = lax.broadcasted_iota(jnp.int32, (1, width), 1)
@@ -139,10 +148,10 @@
         chosen = jnp.where(mine, slices_ref[k], chosen)
         mine_v = jnp.full((1, width), owners_ref[k], jnp.int32) == row
         wanted = jnp.where(mine_v, relabels_ref[k - 1 : k, :], wanted)
-    places = lax.broadcasted_iota(jnp.int32, (width, width), 0)
-    onehot_v[...] = jnp.where(places == wanted, 1.0, 0.0).astype(jnp.bfloat16)
-    loads[0].wait()
-    loads[1].wait()
+    bonds = lax.broadcasted_iota(jnp.int32, (width, width), 0)
+    onehot_v[...] = jnp.where(bonds == wanted, 1.0, 0.0).astype(jnp.bfloat16)
+    for load in loads[small:pools]:
+        load.wait()
 
     def use_of(holder):
         use = count
@@ -181,7 +190,7 @@
         return own_copy(step ^ 2)
 
     def far_copy(slot, step, part):
-        rows = pl.ds(part * group, group)
+        rows = pl.ds(part * 2 * group // PARTS, 2 * group // PARTS)
         return copy(
             slots[slot][step].at[0, rows],
             slots[slot][step].at[1, rows],
@@ -192,7 +201,7 @@
 
     def side_copy(slot, step, part):
         to = step ^ 1
-        rows = pl.ds(part * group, group)
+        rows = pl.ds(part * 2 * group // PARTS, 2 * group // PARTS)
         return copy(
             slots[slot][step].at[1, rows],
             slots[slot][to].at[1, rows],
@@ -203,7 +212,7 @@
 
     def pass_copy(slot, step, part):
         to = step ^ 2
-        rows = pl.ds(part * group, group)
+        rows = pl.ds(part * 2 * group // PARTS, 2 * group // PARTS)
         return copy(
             slots[slot][step].at[1, rows],
             slots[slot][to].at[1, rows],
@@ -302,10 +311,10 @@
     shared = bases[: -(len(bases) // 2) or None]
     direct = bases[len(shared) :]
     late_far = shared + [step for base in direct for step in (base, base + 1)]
-    halves = range(2)
+    halves = range(PARTS)
     journey = [(0, base, part) for base in bases for part in halves]
     journey += [(1, step, part) for step in late_far for part in halves]
-    early_halves = 2 * len(bases)
+    early_halves = PARTS * len(bases)
     sided = {(0, base) for base in bases} | {(1, base) for base in shared}
     passes = []
 
@@ -320,7 +329,7 @@
             side_copy(slot, step, part).start()
         hand_on(slot, step, part)
         far_copy(slot, step, part).wait_send()
-        if number == early_halves - 2:
+        if number == early_halves - 1:
             for later in journey[early_halves:]:
                 far_copy(*later).start()
 
@@ -343,8 +352,8 @@
         place_own(base)
         for part in halves:
             far_copy(0, base, part).start()
-    loads[2].wait()
-    loads[3].wait()
+    for load in loads[pools:]:
+        load.wait()
     odd_left = list(bases)
 
     def make_odd():
@@ -355,12 +364,12 @@
             own_copy(base + 1).start()
 
     make_odd()
-    arrived = 0
     advance(0)
     while odd_left:
         make_odd()
-    advance(1)
-    arrived = 2
+    for arrived in range(1, PARTS):
+        advance(arrived)
+    arrived = PARTS
     for step in range(n_col):
         if step not in bases:
             place_own(step)
@@ -414,6 +423,15 @@
     while waiting:
         finish_shared()
 
+    for step in range(n_col):
+        own_copy(step).wait_send()
+    for slot, step in sorted(sided):
+        for part in halves:
+            side_copy(slot, step, part).wait_send()
+    for slot, step, part in passes:
+        pass_copy(slot, step, part).wait_send()
+    for apart in range(1, n_col):
+        swap_any(0, apart).wait_send()
     for k in range(2, count):
         for step in range(n_col):
             last_v[step * 2 * group : (step + 1) * 2 * group, :] = branch_of(k, step)
@@ -428,14 +446,7 @@
                 out_ref[0, rows_of(step), :] = real
                 out_ref[1, rows_of(step), :] = imaginary
 
-    for step in range(n_col):
-        own_copy(step).wait_send()
-    for slot, step in sorted(sided):
-        for part in halves:
-            side_copy(slot, step, part).wait_send()
-    for slot, step, part in passes:
-        pass_copy(slot, step, part).wait_send()
-    for turn in range(count - 1):
+    for turn in range(1, count - 1):
         for apart in range(1, n_col):
             swap_any(turn, apart).wait_send()
 
@@ -465,14 +476,14 @@
             pltpu.VMEM((width, 2 * open_size), dtype),
             pltpu.VMEM((count - 1, width, 2 * open_size), dtype),
             pltpu.VMEM((count - 1, n_col, group, 2 * open_size), dtype),
-            dma((7,)),
+            dma((7 + 2 * right_pool.shape[1],)),
             dma((n_col,)),
             dma((n_col,)),
-            dma((2, n_col, 2)),
-            dma((2, n_col, 2)),
-            dma((2, n_col, 2)),
-            dma((2, n_col, 2)),
-            dma((2, n_col, 2)),
+            dma((2, n_col, PARTS)),
+            dma((2, n_col, PARTS)),
+            dma((2, n_col, PARTS)),
+            dma((2, n_col, PARTS)),
+            dma((2, n_col, PARTS)),
             dma((count - 1, n_col)),
             dma((count - 1, n_col)),
         ],

time: 37.6 us -> 37.8 us (level)
  no operation moved by 1% of the time
where the time goes in v7:
time: 37.8 us; the launch traced here: 37.7 us
  Pallas kernels  36 us (95%)
  local copies, waits for them, and re-layouts  1.67 us (4%)
    pallas_call x1, Pallas kernels, fused_body(): pl.pallas_call(functools.partial(fused_kernel, n_col), out_shape=jax.Shap...  36 us
    unnamed x1, local copies, waits for them, and re-layouts  1.67 us

profile of v7, /device:TPU:0, one launch (start us, length us, event | category | flops | bytes accessed | tf_op | source)
XLA Modules:
  0.0 37.7 jit_solution(6553696465349939486)
XLA Ops:
  0.0 36.0 %shard_map.64 = bf16[2,512,128]{2,1,0:T(8,128)(2,1)} custom-call(s32[3]{0:T(128)} %owners_hbm.1, s32[3]{0:T(128)} %slices_hbm.1, s32[2,512]{1,0:T(2,128)} %relabels_hbm.1, bf16[2,512,128]{2,1,0:T(8,128)(2,1)} %stem_hbm.1, bf16[1,2,512,512]{3,2,1,0:T(8,128)(2,1)} %left_hbm.1, bf16[1,2,2,512,512]{4,3,2,1,0:T(8,128)(2,1)} %right_hbm.1), custom_call_target="tpu_custom_call" | custom-call | flops 2952790016 | bytes 3670016 | tf_op jit(solution)/shard_map/pallas_call | solution.py:460
  36.0 1.7 %copy.8 = bf16[2,512,128]{2,1,0:T(8,128)(2,1)} copy(bf16[2,512,128]{2,1,0:T(8,128)(2,1)} %shard_map.64) | data formatting | bytes 524288

commit v8 on v7

--- a/solution.py
+++ b/solution.py
@@ -8,7 +8,8 @@
 from jax.sharding import PartitionSpec as P
 
 MESH = pl.DeviceIdType.MESH
-PARTS = 1
+LANES = 128
+PARTS = 2
 
 
 def complex_product(first, second):
@@ -148,8 +149,9 @@
         chosen = jnp.where(mine, slices_ref[k], chosen)
         mine_v = jnp.full((1, width), owners_ref[k], jnp.int32) == row
         wanted = jnp.where(mine_v, relabels_ref[k - 1 : k, :], wanted)
-    bonds = lax.broadcasted_iota(jnp.int32, (width, width), 0)
-    onehot_v[...] = jnp.where(bonds == wanted, 1.0, 0.0).astype(jnp.bfloat16)
+    column = jnp.transpose(jnp.broadcast_to(wanted, (LANES, width)))[:, :1]
+    bonds = lax.broadcasted_iota(jnp.int32, (width, width), 1)
+    onehot_v[...] = jnp.where(bonds == column, 1.0, 0.0).astype(jnp.bfloat16)
     for load in loads[small:pools]:
         load.wait()
 
@@ -254,10 +256,9 @@
             middle, stop = start + group, start + 2 * group
             rows.append(by_real[start:middle] - by_imag[middle:stop])
             rows.append(by_imag[start:middle] + by_real[middle:stop])
-        moved = lax.dot_general(
+        moved = jnp.dot(
             jnp.concatenate(rows, axis=0).astype(jnp.bfloat16),
             onehot_v[...],
-            (((1,), (1,)), ((), ())),
             preferred_element_type=jnp.float32,
         ).astype(jnp.bfloat16)
         pair[first][0] = moved[: 2 * group]
@@ -329,7 +330,7 @@
             side_copy(slot, step, part).start()
         hand_on(slot, step, part)
         far_copy(slot, step, part).wait_send()
-        if number == early_halves - 1:
+        if number == early_halves - 2:
             for later in journey[early_halves:]:
                 far_copy(*later).start()
 

time: 37.8 us -> 37.6 us (level)
  no operation moved by 1% of the time
where the time goes in v8:
time: 37.6 us; the launch traced here: 37.4 us
  Pallas kernels  35.7 us (95%)
  local copies, waits for them, and re-layouts  1.67 us (4%)
    pallas_call x1, Pallas kernels, fused_body(): pl.pallas_call(functools.partial(fused_kernel, n_col), out_shape=jax.Shap...  35.7 us
    unnamed x1, local copies, waits for them, and re-layouts  1.67 us

profile of v8, /device:TPU:0, one launch (start us, length us, event | category | flops | bytes accessed | tf_op | source)
XLA Modules:
  0.0 37.4 jit_solution(6096428152491270968)
XLA Ops:
  0.0 35.7 %shard_map.64 = bf16[2,512,128]{2,1,0:T(8,128)(2,1)} custom-call(s32[3]{0:T(128)} %owners_hbm.1, s32[3]{0:T(128)} %slices_hbm.1, s32[2,512]{1,0:T(2,128)} %relabels_hbm.1, bf16[2,512,128]{2,1,0:T(8,128)(2,1)} %stem_hbm.1, bf16[1,2,512,512]{3,2,1,0:T(8,128)(2,1)} %left_hbm.1, bf16[1,2,2,512,512]{4,3,2,1,0:T(8,128)(2,1)} %right_hbm.1), custom_call_target="tpu_custom_call" | custom-call | flops 2952790016 | bytes 3670016 | tf_op jit(solution)/shard_map/pallas_call | solution.py:461
  35.8 1.7 %copy.8 = bf16[2,512,128]{2,1,0:T(8,128)(2,1)} copy(bf16[2,512,128]{2,1,0:T(8,128)(2,1)} %shard_map.64) | data formatting | bytes 524288

commit v9 on v8

--- a/solution.py
+++ b/solution.py
@@ -107,12 +107,10 @@
 
     def partner(step):
         other = at_distance(step)
-        return other + core * (flip(other, 2) - other)
+        return other + core * (flip(other, 4) - other)
 
     def distance(step):
-        return step - 2 * core if step & 2 else step + 2 * core
-
-    beside = at_distance(1)
+        return step - 4 * core if step & 4 else step + 4 * core
 
     places = [
         (owners_hbm, owners_ref),
@@ -183,13 +181,13 @@
         )
 
     def own_copy(step):
-        to = step ^ 2
+        to = step ^ 4
         return copy(
             pair[step].at[0], pair[to].at[1], own_send.at[step], own_recv.at[to], (sibling, col)
         )
 
     def own_arrival(step):
-        return own_copy(step ^ 2)
+        return own_copy(step ^ 4)
 
     def far_copy(slot, step, part):
         rows = pl.ds(part * 2 * group // PARTS, 2 * group // PARTS)
@@ -201,19 +199,19 @@
             (across, col),
         )
 
-    def side_copy(slot, step, part):
-        to = step ^ 1
+    def side_copy(slot, step, hop, part):
+        to = step ^ hop
         rows = pl.ds(part * 2 * group // PARTS, 2 * group // PARTS)
         return copy(
             slots[slot][step].at[1, rows],
             slots[slot][to].at[1, rows],
-            side_send.at[slot, step, part],
+            side_send.at[slot, to, part],
             far_recv.at[slot, to, part],
-            (row, beside),
+            (row, at_distance(hop)),
         )
 
     def pass_copy(slot, step, part):
-        to = step ^ 2
+        to = step ^ 4
         rows = pl.ds(part * 2 * group // PARTS, 2 * group // PARTS)
         return copy(
             slots[slot][step].at[1, rows],
@@ -294,8 +292,8 @@
     def send_on(k, step, real, imaginary):
         sends[k, step, :, :open_size] = real
         sends[k, step, :, open_size:] = imaginary
-        if step in (0, 2):
-            stays = core == step // 2
+        if step in (0, 4):
+            stays = core == step // 4
 
             @pl.when(stays)
             def _():
@@ -308,15 +306,17 @@
         else:
             swap_copy(k, step).start()
 
-    bases = list(range(n_col - 4, -1, -4))
-    shared = bases[: -(len(bases) // 2) or None]
-    direct = bases[len(shared) :]
-    late_far = shared + [step for base in direct for step in (base, base + 1)]
+    bases = list(range(n_col - 8, -1, -8))
     halves = range(PARTS)
-    journey = [(0, base, part) for base in bases for part in halves]
-    journey += [(1, step, part) for step in late_far for part in halves]
-    early_halves = PARTS * len(bases)
-    sided = {(0, base) for base in bases} | {(1, base) for base in shared}
+    journey = [
+        (slot, base + step, part)
+        for slot in range(2)
+        for base in bases
+        for step in (0, 3)
+        for part in halves
+    ]
+    early_halves = len(journey) // 2
+    sides = [(slot, base, hop) for slot in range(2) for base in bases for hop in (1, 2)]
     passes = []
 
     def hand_on(slot, step, part):
@@ -326,8 +326,9 @@
     def advance(number):
         slot, step, part = journey[number]
         far_copy(slot, step, part).wait_recv()
-        if (slot, step) in sided:
-            side_copy(slot, step, part).start()
+        for hop in (1, 2):
+            if (slot, step, hop) in sides:
+                side_copy(slot, step, hop, part).start()
         hand_on(slot, step, part)
         far_copy(slot, step, part).wait_send()
         if number == early_halves - 2:
@@ -341,94 +342,75 @@
 
     def from_sibling(slot, step):
         for part in halves:
-            pass_copy(slot, step ^ 2, part).wait_recv()
-
-    for place, base in enumerate(bases):
-        make_own(base + 2, base)
-        if place == 0:
+            pass_copy(slot, step ^ 4, part).wait_recv()
+
+    def make_pair(step):
+        make_own(step + 4, step)
+        if not entered:
             pl.semaphore_wait(barrier, len(greet))
-        own_copy(base + 2).start()
-        own_copy(base).start()
+            entered.append(True)
+        own_copy(step + 4).start()
+        own_copy(step).start()
+
+    entered = []
     for base in bases:
-        place_own(base)
-        for part in halves:
-            far_copy(0, base, part).start()
+        make_pair(base)
+        make_pair(base + 3)
+    for base in bases:
+        for step in (base, base + 3):
+            place_own(step)
+            for part in halves:
+                far_copy(0, step, part).start()
     for load in loads[pools:]:
         load.wait()
-    odd_left = list(bases)
-
-    def make_odd():
-        if odd_left:
-            base = odd_left.pop(0)
-            make_own(base + 3, base + 1)
-            own_copy(base + 3).start()
-            own_copy(base + 1).start()
-
-    make_odd()
-    advance(0)
-    while odd_left:
-        make_odd()
-    for arrived in range(1, PARTS):
-        advance(arrived)
-    arrived = PARTS
-    for step in range(n_col):
-        if step not in bases:
-            place_own(step)
+    for base in bases:
+        make_pair(base + 1)
+        make_pair(base + 2)
+
+    arrived = 0
+
+    def arrive():
+        nonlocal arrived
+        for _ in halves:
+            advance(arrived)
+            arrived += 1
+
+    def apply_slot(slot, base, state, first):
+        if first:
+            apply_and_send(slot, base, state)
+            from_sibling(slot, base + 4)
+            apply_and_send(slot, base + 4, state)
+            return
+        arrive()
+        apply_and_send(slot, base + 3, state)
+        for step in (base + 1, base + 2):
+            from_beside(slot, step)
+            apply_and_send(slot, step, state)
+        for step in (base + 7, base + 5, base + 6):
+            from_sibling(slot, step)
+            apply_and_send(slot, step, state)
+
+    for base in bases:
+        arrive()
+        if base == bases[0]:
+            for step in range(n_col):
+                if step % 8 not in (0, 3):
+                    place_own(step)
+        apply_slot(0, base, state0[...], True)
+        apply_slot(0, base, state0[...], False)
     for place, base in enumerate(bases):
-        if place > 0:
-            for part in halves:
-                advance(arrived)
-                arrived += 1
-        apply_and_send(0, base, state0[...])
-        from_sibling(0, base + 2)
-        apply_and_send(0, base + 2, state0[...])
-    for place, base in enumerate(bases):
-        from_beside(0, base + 1)
-        apply_and_send(0, base + 1, state0[...])
-        from_sibling(0, base + 3)
-        apply_and_send(0, base + 3, state0[...])
-        if place < len(shared):
-            for part in halves:
-                advance(arrived)
-                arrived += 1
-
-    for apart in range(1, n_col):
-        swap_any(0, apart).wait_recv()
-
-    def apply_late(k, step):
-        apply_and_send(k, step, states[k - 1])
-
-    for base in shared:
-        from_sibling(1, base + 2)
-        apply_late(1, base)
-        apply_late(1, base + 2)
-    waiting = list(shared)
-
-    def finish_shared():
-        if waiting:
-            base = waiting.pop(0)
-            from_beside(1, base + 1)
-            apply_late(1, base + 1)
-            from_sibling(1, base + 3)
-            apply_late(1, base + 3)
-
-    for base in direct:
-        for step in (base, base + 1):
-            for part in halves:
-                advance(arrived)
-                arrived += 1
-            apply_late(1, step)
-            from_sibling(1, step + 2)
-            apply_late(1, step + 2)
-            finish_shared()
-    while waiting:
-        finish_shared()
+        arrive()
+        if place == 0:
+            for apart in range(1, n_col):
+                swap_any(0, apart).wait_recv()
+        apply_slot(1, base, states[0], True)
+        apply_slot(1, base, states[0], False)
 
     for step in range(n_col):
         own_copy(step).wait_send()
-    for slot, step in sorted(sided):
+    for slot, step, hop in sides:
         for part in halves:
-            side_copy(slot, step, part).wait_send()
+            side_copy(slot, step, hop, part).wait_send()
     for slot, step, part in passes:
         pass_copy(slot, step, part).wait_send()
     for apart in range(1, n_col):
@@ -501,7 +483,7 @@
 
 def solution(mesh):
     n_row, n_col = mesh.shape["row"], mesh.shape["col"]
-    few = n_row == 4 and n_col >= 4 and n_col & (n_col - 1) == 0
+    few = n_row == 4 and n_col >= 8 and n_col & (n_col - 1) == 0
     body = functools.partial(fused_body, n_col) if few else plain_body
     in_specs = (
         P(None, None, ("row", "col")),

time: 37.6 us -> 35.1 us (0.934)
  Pallas kernels: 35.7 us -> 33.3 us
    pallas_call x1, Pallas kernels: 35.7 us -> 33.3 us  [fused_body(): pl.pallas_call(functools.partial(fused_kernel, n_col), out_shape=jax.Shap...]
where the time goes in v9:
time: 35.1 us; the launch traced here: 34.9 us
  Pallas kernels  33.3 us (95%)
  local copies, waits for them, and re-layouts  1.67 us (5%)
    pallas_call x1, Pallas kernels, fused_body(): pl.pallas_call(functools.partial(fused_kernel, n_col), out_shape=jax.Shap...  33.3 us
    unnamed x1, local copies, waits for them, and re-layouts  1.67 us

profile of v9, /device:TPU:0, one launch (start us, length us, event | category | flops | bytes accessed | tf_op | source)
XLA Modules:
  0.0 34.9 jit_solution(13703674852408791046)
XLA Ops:
  0.0 33.3 %shard_map.64 = bf16[2,512,128]{2,1,0:T(8,128)(2,1)} custom-call(s32[3]{0:T(128)} %owners_hbm.1, s32[3]{0:T(128)} %slices_hbm.1, s32[2,512]{1,0:T(2,128)} %relabels_hbm.1, bf16[2,512,128]{2,1,0:T(8,128)(2,1)} %stem_hbm.1, bf16[1,2,512,512]{3,2,1,0:T(8,128)(2,1)} %left_hbm.1, bf16[1,2,2,512,512]{4,3,2,1,0:T(8,128)(2,1)} %right_hbm.1), custom_call_target="tpu_custom_call" | custom-call | flops 2952790016 | bytes 3670016 | tf_op jit(solution)/shard_map/pallas_call | solution.py:443
  33.3 1.7 %copy.8 = bf16[2,512,128]{2,1,0:T(8,128)(2,1)} copy(bf16[2,512,128]{2,1,0:T(8,128)(2,1)} %shard_map.64) | data formatting | bytes 524288

commit v10 on v9

--- a/solution.py
+++ b/solution.py
@@ -312,11 +312,11 @@
         (slot, base + step, part)
         for slot in range(2)
         for base in bases
-        for step in (0, 3)
+        for step in (3, 0)
         for part in halves
     ]
     early_halves = len(journey) // 2
-    sides = [(slot, base, hop) for slot in range(2) for base in bases for hop in (1, 2)]
+    sides = [(slot, base + 3, hop) for slot in range(2) for base in bases for hop in (1, 2)]
     passes = []
 
     def hand_on(slot, step, part):
@@ -354,10 +354,10 @@
 
     entered = []
     for base in bases:
+        make_pair(base + 3)
         make_pair(base)
-        make_pair(base + 3)
     for base in bases:
-        for step in (base, base + 3):
+        for step in (base + 3, base):
             place_own(step)
             for part in halves:
                 far_copy(0, step, part).start()
@@ -377,16 +377,16 @@
 
     def apply_slot(slot, base, state, first):
         if first:
-            apply_and_send(slot, base, state)
-            from_sibling(slot, base + 4)
-            apply_and_send(slot, base + 4, state)
+            apply_and_send(slot, base + 3, state)
+            from_sibling(slot, base + 7)
+            apply_and_send(slot, base + 7, state)
             return
         arrive()
-        apply_and_send(slot, base + 3, state)
+        apply_and_send(slot, base, state)
         for step in (base + 1, base + 2):
             from_beside(slot, step)
             apply_and_send(slot, step, state)
-        for step in (base + 7, base + 5, base + 6):
+        for step in (base + 4, base + 5, base + 6):
             from_sibling(slot, step)
             apply_and_send(slot, step, state)
 

time: 35.1 us -> 35.1 us (level)
  no operation moved by 1% of the time
where the time goes in v10:
time: 35.1 us; the launch traced here: 34.9 us
  Pallas kernels  33.2 us (95%)
  local copies, waits for them, and re-layouts  1.67 us (5%)
    pallas_call x1, Pallas kernels, fused_body(): pl.pallas_call(functools.partial(fused_kernel, n_col), out_shape=jax.Shap...  33.2 us
    unnamed x1, local copies, waits for them, and re-layouts  1.67 us

profile of v10, /device:TPU:0, one launch (start us, length us, event | category | flops | bytes accessed | tf_op | source)
XLA Modules:
  0.0 34.9 jit_solution(17668827609982945078)
XLA Ops:
  0.0 33.2 %shard_map.64 = bf16[2,512,128]{2,1,0:T(8,128)(2,1)} custom-call(s32[3]{0:T(128)} %owners_hbm.1, s32[3]{0:T(128)} %slices_hbm.1, s32[2,512]{1,0:T(2,128)} %relabels_hbm.1, bf16[2,512,128]{2,1,0:T(8,128)(2,1)} %stem_hbm.1, bf16[1,2,512,512]{3,2,1,0:T(8,128)(2,1)} %left_hbm.1, bf16[1,2,2,512,512]{4,3,2,1,0:T(8,128)(2,1)} %right_hbm.1), custom_call_target="tpu_custom_call" | custom-call | flops 2952790016 | bytes 3670016 | tf_op jit(solution)/shard_map/pallas_call | solution.py:443
  33.3 1.7 %copy.8 = bf16[2,512,128]{2,1,0:T(8,128)(2,1)} copy(bf16[2,512,128]{2,1,0:T(8,128)(2,1)} %shard_map.64) | data formatting | bytes 524288
